TPU v7x, 256 devices: a whole 4x4x8 slice. The times are simulated.
256 devices in a mesh: sector: 16 (over y, x), box: 16 (over z, core).
Axes of the slice: x: 4, y: 4, z: 8, core: 2. Of those that a mesh axis runs over, the one named last changes fastest.
Arguments:
- positions: float32 [3, 16, 1024, 128], P(None, 'sector', 'box'), may hold values from -0.9 to 0.9
- strengths: float32 [3, 16, 1024, 128], P(None, 'sector', 'box'), may hold values from -6 to 6
- counts: int32 [16, 1024], P('sector', 'box'), may hold values from 1 to 128
- cross_slot: int32 [16, 4096], P('sector', 'box'), may hold values from 0 to 8191, as said below
- arrive_box: int32 [16, 4096], P('sector', 'box'), may hold values from 0 to 63
- il_source: int32 [16, 1024, 16], P('sector', 'box'), may hold values from 0 to 63
- il_class: int32 [16, 1024, 16], P('sector', 'box'), may hold values from 0 to 3
- m2m: bfloat16 [4, 441, 441], replicated, may hold values from -0.125 to 0.125
- m2l_leaf: bfloat16 [4, 441, 441], replicated, may hold values from -0.0625 to 0.0625
- tree_up: bfloat16 [2, 441, 441], replicated, may hold values from -0.21875 to 0.21875
- tree_m2l: bfloat16 [2, 441, 441], replicated, may hold values from -0.25 to 0.25
- m2l_sector: bfloat16 [15, 441, 441], replicated, may hold values from -0.078125 to 0.078125
Outputs:
- new_positions: float32 [3, 16, 1024, 128], P(None, 'sector', 'box')
- velocity: float32 [3, 16, 1024, 128], P(None, 'sector', 'box')
Inputs may be any that keep to these rules, and one draw needn't show every extreme that they name: `cross_slot`: within one block's 256 entries the slot numbers are distinct; a slot beyond its box's count carries nothing.
All inputs are finite; a program needn't handle non-finite values.
Results may differ from a plain program's by a relative error of at most 0.006.
Values may be sent and summed in bfloat16 or wider, within the bound.
A program may use at most 128 MiB of HBM per device.

v0:
```python
import math
import jax
import jax.numpy as jnp
from jax import lax
from jax.sharding import PartitionSpec as P

TERMS = 21
LEVELS_DEV = 3
NCLASS = 4
DELTA_SQ = 0.25
TIME_STEP = 0.02
INV_FOUR_PI = 1.0 / (4.0 * math.pi)
HIGHEST_PRECISION = lax.Precision.HIGHEST
OFFSETS = ((0.0, 0.0, 0.0), (0.0, 0.0, -2.0), (0.0, 0.0, 2.0), (-2.0, 0.0, 0.0), (2.0, 0.0, 0.0))


def with_halo(array, sides, width, wrap):
    for axis, dim in sides:
        devices, length = (lax.axis_size(axis), array.shape[dim])
        up = [(i, (i + 1) % devices) for i in range(devices if wrap else devices - 1)]
        down = [(j, i) for i, j in up]
        last = lax.slice_in_dim(array, length - width, length, axis=dim)
        first = lax.slice_in_dim(array, 0, width, axis=dim)
        before = lax.ppermute(last, axis, up)
        after = lax.ppermute(first, axis, down)
        array = jnp.concatenate([before, array, after], axis=dim)
    return array


def partner_2(block, axis, distance):
    count = lax.axis_size(axis)
    route = []
    for low in range(count):
        high = low | 1 << distance
        if high != low and high < count:
            route += [(low, high), (high, low)]
    return lax.ppermute(block, axis, route)


def passed_along(array, axis, by):
    devices = lax.axis_size(axis)
    return lax.ppermute(array, axis, [(i, (i + by) % devices) for i in range(devices)])


def chebyshev(coordinate):
    scaled = 0.5 * coordinate
    series = [jnp.ones_like(scaled), scaled]
    for order in range(2, TERMS):
        series.append(2.0 * scaled * series[-1] - series[-2])
    return jnp.stack(series[:TERMS])


def multipoles(cheb_a, cheb_b, weights):
    weighted = weights[:, None] * cheb_a[None]
    return jnp.einsum("cjnp,knp->ncjk", weighted, cheb_b, precision=HIGHEST_PRECISION)


def evaluate(local, cheb_a, cheb_b):
    shaped = local.reshape(local.shape[0], 3, TERMS, TERMS)
    partial_sum = jnp.einsum("ncjk,knp->cjnp", shaped, cheb_b, precision=HIGHEST_PRECISION)
    return jnp.sum(partial_sum * cheb_a[None], axis=1) / TERMS


def pair_velocity(target, source, weight, offset):
    delta_x = target[0][:, :, None] - (source[0][:, None, :] + offset[0])
    delta_y = target[1][:, :, None] - (source[1][:, None, :] + offset[1])
    delta_z = target[2][:, :, None] - (source[2][:, None, :] + offset[2])
    radius_sq = delta_x * delta_x + delta_y * delta_y + delta_z * delta_z + DELTA_SQ
    inverse = INV_FOUR_PI / (radius_sq * jnp.sqrt(radius_sq))
    weight_x = weight[0][:, None, :]
    weight_y = weight[1][:, None, :]
    weight_z = weight[2][:, None, :]
    speed_x = jnp.sum(inverse * (weight_y * delta_z - weight_z * delta_y), axis=2)
    speed_y = jnp.sum(inverse * (weight_z * delta_x - weight_x * delta_z), axis=2)
    speed_z = jnp.sum(inverse * (weight_x * delta_y - weight_y * delta_x), axis=2)
    return jnp.stack([speed_x, speed_y, speed_z])


def near_field(places, weights):
    box_count, slots = (places.shape[1], places.shape[2])
    stacked = jnp.concatenate([places, weights], axis=0)[:, None]
    beside = with_halo(stacked.astype(jnp.bfloat16), (("sector", 1),), 1, True).astype(
        stacked.dtype
    )
    along = with_halo(stacked.astype(jnp.bfloat16), (("box", 2),), 1, False).astype(stacked.dtype)
    sources = [stacked[:, 0], along[:, 0, :box_count], along[:, 0, 2:], beside[:, 0], beside[:, 2]]
    block = math.gcd(box_count, 64)
    block_count = box_count // block

    def arrange(array):
        return array.reshape(array.shape[0], block_count, block, slots).transpose(1, 0, 2, 3)

    inputs = (arrange(places),) + tuple((arrange(item) for item in sources))

    def block_velocity(items):
        summed = jnp.zeros_like(items[0])
        for index in range(5):
            summed = summed + pair_velocity(
                items[0], items[1 + index][:3], items[1 + index][3:], OFFSETS[index]
            )
        return summed

    result = lax.map(block_velocity, inputs)
    return result.transpose(1, 0, 2, 3).reshape(3, box_count, slots)


def merge_pair(current, partner, side_bit, tree_up):
    lower_node = jnp.where(side_bit == 0, current, partner)
    upper_node = jnp.where(side_bit == 0, partner, current)
    merged = jnp.dot(lower_node, tree_up[0], preferred_element_type=jnp.float32) + jnp.dot(
        upper_node, tree_up[1], preferred_element_type=jnp.float32
    )
    return merged.astype(jnp.bfloat16)


def far_field(
    places,
    weights,
    arrival_terms,
    il_source,
    il_class,
    m2m,
    m2l_leaf,
    tree_up,
    tree_m2l,
    m2l_sector,
):
    box_count = places.shape[1]
    coef = TERMS * TERMS
    cheb_a = chebyshev(places[0])
    cheb_b = chebyshev(places[1])
    leaf = (
        (multipoles(cheb_a, cheb_b, weights) + arrival_terms)
        .reshape(box_count, 3, coef)
        .astype(jnp.bfloat16)
    )
    upward = leaf
    for depth in range(LEVELS_DEV):
        grouped = upward.reshape(-1, 4, 3, coef)
        upward = jnp.einsum(
            "gocx,oxy->gcy", grouped, m2m, preferred_element_type=jnp.float32
        ).astype(jnp.bfloat16)
    block_root = upward[0]
    box_index = lax.axis_index("box")
    depth_count = lax.axis_size("box").bit_length() - 1
    siblings = []
    side_bits = []
    current = block_root
    for depth in range(depth_count):
        partner = partner_2(current, "box", depth)
        side_bit = box_index >> depth & 1
        siblings.append(partner)
        side_bits.append(side_bit)
        current = merge_pair(current, partner, side_bit, tree_up)
    sector_index = lax.axis_index("sector")
    sector_count = lax.axis_size("sector")
    piece = lax.all_gather(current[None], "sector", axis=0, tiled=True)
    source_ids = jnp.arange(piece.shape[0], dtype=jnp.int32)
    distance = (source_ids - sector_index) % sector_count
    matrices = m2l_sector[jnp.maximum(distance - 1, 0)]
    masked_piece = jnp.where((distance != 0)[:, None, None], piece, jnp.zeros_like(piece))
    far_sum = jnp.einsum("ncx,nxy->cy", masked_piece, matrices, preferred_element_type=jnp.float32)
    local = far_sum.astype(jnp.bfloat16)
    for depth in reversed(range(depth_count)):
        up_side = lax.dynamic_index_in_dim(tree_up, side_bits[depth], 0, keepdims=False)
        cross_side = lax.dynamic_index_in_dim(tree_m2l, side_bits[depth], 0, keepdims=False)
        downward = jnp.einsum(
            "cy,xy->cx", local, up_side, preferred_element_type=jnp.float32
        ) + jnp.dot(siblings[depth], cross_side, preferred_element_type=jnp.float32)
        local = downward.astype(jnp.bfloat16)
    parent_local = local[None]
    child = jnp.zeros((box_count, 3, coef), jnp.float32)
    for depth in range(LEVELS_DEV):
        child = jnp.einsum(
            "gcy,oxy->gocx", parent_local, m2m, preferred_element_type=jnp.float32
        ).reshape(-1, 3, coef)
        if depth + 1 < LEVELS_DEV:
            parent_local = child.astype(jnp.bfloat16)
    box_ids = jnp.arange(box_count, dtype=jnp.int32)
    source_hit = (il_source[0][:, :, None] == box_ids[None, None, :]).astype(jnp.bfloat16)
    class_hit = (
        il_class[0][:, :, None] == jnp.arange(NCLASS, dtype=jnp.int32)[None, None, :]
    ).astype(jnp.bfloat16)
    pair_counts = jnp.einsum(
        "bic,bis->cbs", class_hit, source_hit, preferred_element_type=jnp.float32
    ).astype(jnp.bfloat16)
    presum = jnp.einsum(
        "cbs,sx->cbx",
        pair_counts,
        leaf.reshape(box_count, 3 * coef),
        preferred_element_type=jnp.float32,
    )
    presum = presum.astype(jnp.bfloat16).reshape(NCLASS, box_count * 3, coef)
    translated = jnp.einsum(
        "cnx,cxy->ny", presum, m2l_leaf, preferred_element_type=jnp.float32
    ).reshape(box_count, 3, coef)
    return evaluate(child + translated, cheb_a, cheb_b)


def per_device(
    positions,
    strengths,
    counts,
    cross_slot,
    arrive_box,
    il_source,
    il_class,
    m2m,
    m2l_leaf,
    tree_up,
    tree_m2l,
    m2l_sector,
):
    box_count, slots = (positions.shape[2], positions.shape[3])
    slot_ids = jnp.arange(slots, dtype=jnp.int32)
    present = (slot_ids[None, :] < counts[0][:, None]).astype(jnp.float32)
    crossing = cross_slot[0]
    departed = jnp.zeros((box_count * slots,), jnp.float32).at[crossing].set(1.0)
    live = present * (1.0 - departed.reshape(box_count, slots))
    flat_places = positions[:, 0].reshape(3, box_count * slots)
    flat_strength = strengths[:, 0].reshape(3, box_count * slots)
    leave_present = present.reshape(-1)[crossing]
    leaving = jnp.concatenate(
        [flat_places[:, crossing], flat_strength[:, crossing] * leave_present[None]], axis=0
    )
    arrived = passed_along(leaving, "sector", 1)
    arrive_cheb_a = chebyshev(arrived[0][:, None])
    arrive_cheb_b = chebyshev(arrived[1][:, None])
    arrival_each = multipoles(arrive_cheb_a, arrive_cheb_b, arrived[3:6][:, :, None])
    box_ids = jnp.arange(box_count, dtype=jnp.int32)
    landing = (arrive_box[0][None, :] == box_ids[:, None]).astype(jnp.float32)
    arrival_terms = jnp.dot(
        landing, arrival_each.reshape(landing.shape[1], -1), precision=HIGHEST_PRECISION
    )
    arrival_terms = arrival_terms.reshape(box_count, 3, TERMS, TERMS)
    places = positions[:, 0]
    weights = strengths[:, 0] * live[None]
    velocity = jnp.zeros_like(places)
    for substep in range(2):
        near = near_field(places, weights)
        far = far_field(
            places,
            weights,
            arrival_terms,
            il_source,
            il_class,
            m2m,
            m2l_leaf,
            tree_up,
            tree_m2l,
            m2l_sector,
        )
        velocity = near + far
        places = places + TIME_STEP * velocity
    return (places[:, None], velocity[:, None])


def solution(mesh):
    placed = (
        P(None, "sector", "box", None),
        P(None, "sector", "box", None),
        P("sector", "box"),
        P("sector", "box"),
        P("sector", "box"),
        P("sector", "box", None),
        P("sector", "box", None),
        P(),
        P(),
        P(),
        P(),
        P(),
    )
    return jax.shard_map(
        per_device,
        mesh=mesh,
        in_specs=placed,
        out_specs=(P(None, "sector", "box", None), P(None, "sector", "box", None)),
        check_vma=False,
    )
```

profile of v0, /device:TPU:2, one launch (start us, length us, event | category | flops | bytes accessed | tf_op | source)
XLA Modules:
  0.0 371.9 jit_solution(226998493648815140)
XLA Ops:
  1.4 1.6 bitcast_convert_fusion
  3.0 1.4 scatter_custom_fusion
  6.7 2.3 collective-permute-start.3
  9.0 3.4 copy.326
  12.5 2.7 copy.325
  15.2 3.0 gather_fusion.1
  18.2 1.7 gather_fusion.2
  20.1 2.9 gather_fusion
  26.3 3.6 collective-permute-start
  36.4 6.5 %constant_dynamic-slice_fusion.1 = (bf16[1,441,441]{2,0,1:T(2,128)(2,1)}, bf16[1,441,441]{2,0,1:T(2,128)(2,1)}, bf16[1,441,441]{2,0,1:T(2,128)(2,1)}, bf16[1,441...) fusion(bf16[2,441,441]{2,0,1:T(2,128)(2,1)S(1)} %copy-done.2, ...), kind=kLoop, calls=%fused_computation.812 | loop fusion | bytes 4667560 | tf_op jit(solution)/shard_map/jit(dynamic_index_in_dim)/dynamic_slice | solution.py:165
  42.9 4.9 %constant_dynamic-slice_fusion = (bf16[1,441,441]{2,0,1:T(2,128)(2,1)}, bf16[1,441,441]{2,0,1:T(2,128)(2,1)}, bf16[1,441,441]{2,0,1:T(2,128)(2,1)}, bf16[1,441,441]{2,0,1:T(2,128)(2,1)}) fusion(bf16[2,441,441]{2,0,1:T(2,128)(2,1)S(1)} %copy-done.3, s32[]{:T(128)S(6)} %select_n.162, s32[]{:T(128)S(6)} %select_n.161, s32[]{:T(128)S(6)} %select_n.160, ...), kind=kLoop, calls=%fused_computation.811 | loop fusion | bytes 3111712 | tf_op jit(solution)/shard_map/jit(dynamic_index_in_dim)/dynamic_slice | solution.py:166
  50.7 5.4 %fusion.134 = f32[64,3,21,21]{3,2,1,0:T(8,128)S(1)} fusion(f32[21,64,128]{2,0,1:T(8,128)} %copy.323, f32[3,64,128]{2,0,1:T(4,128)} %copy.322, f32[21,64,128,1]{2,1,0,3:T(8,128)} %bitcast.1389), kind=kOutput, calls=%fused_computation.243 | convolution fusion | flops 130572288 | bytes 1813248 | tf_op jit(solution)/shard_map/cjnp,knp->ncjk/dot_general | solution.py:55
  56.6 1.6 copy.329
  58.2 7.0 %gather_fusion.3 = bf16[16,441,441]{2,1,0:T(8,128)(2,1)} fusion(bf16[15,441,441]{2,1,0:T(8,128)(2,1)} %param.23, s32[1024]{0:T(1024)} %pad_clamp_fusion), kind=kCustom, calls=%fused_computation.3 | custom fusion | bytes 12446848 | tf_op jit(solution)/shard_map/gather | solution.py:160
  67.9 2.9 dot_general.193
  70.8 3.3 add_convert_fusion.1
  74.1 1.7 copy.330
  75.8 2.8 convert_element_type.236
  78.6 1.6 fusion.189
  83.6 1.9 collective-permute-start.6
  85.5 1.7 collective-permute-done.6
  87.5 4.4 %collective-permute-start.7 = (bf16[3,441]{1,0:T(4,128)(2,1)S(1)}, bf16[3,441]{1,0:T(4,128)(2,1)S(1)}, u32[]{:S(2)}, u32[]{:S(2)}) collective-permute-start(bf16[3,441]{1,0:T(4,128)(2,1)S(1)} %fusion.240), channel_id=1, source_target_pairs={{0,4},{4,0},{1,5},{5,1},{2,6},{6,2},{3,7},{7,3},{8,12},{12,8},{9,1... | collective-permute-start | bytes 7946 | tf_op jit(solution)/shard_map/ppermute | solution.py:37
  91.9 25.5 %fusion.45 = (f32[64,128]{1,0:T(8,128)}, f32[64,128]{1,0:T(8,128)}, f32[64,128]{1,0:T(8,128)}, f32[64,128]{1,0:T(8,128)}, f32[64,128]{1,0:T(8,128)}, /*index=5*/f32[64,128]{1,0:T(8,128)}) fusion(f32[64,128]{1,0:T(8,128)S(1)} %get-tuple-element.166, f32[64,128]{1,0:T(8,128)S(1)} %get-tuple-element.167, f32[64,128]{1,0:T(8,128)S(1)} %get-tuple-element.168, ...), kind=kLoop, calls=%fused_computation.150 | loop fusion | flops 54476800 | bytes 688128 | tf_op jit(solution)/shard_map/while/body/eval_jaxpr/reduce_sum | solution.py:73
  119.2 3.4 collective-permute-start.8
  124.0 1.7 reshape.4841
  125.7 2.6 copy.356
  130.0 25.7 %all-gather.2 = bf16[16,3,441]{2,1,0:T(4,128)(2,1)S(1)} all-gather(bf16[1,3,441]{2,1,0:T(4,128)(2,1)S(1)} %fusion.266), channel_id=2, replica_groups=mesh['sector'=16,'box'=16] {'sector'}, dimensions={0}, use_global_device_ids=true | all-gather | bytes 44982 | tf_op jit(solution)/shard_map/all_gather | solution.py:157
  155.7 4.6 %fusion.262 = f32[3,441]{1,0:T(4,128)S(1)} fusion(bf16[16,441,441]{2,1,0:T(8,128)(2,1)} %gather_fusion.3, bf16[1,441,441]{2,0,1:T(2,128)(2,1)} %get-tuple-element.125, bf16[16,3,441]{2,1,0:T(4,128)(2,1)S(1)} %all-gather.2, pred[16]{0:T(512)(128)(4,1)} %fusion.434), kind=kOutput, calls=%fused_computation.344 | convolution fusion | flops 19859554 | bytes 6659998 | tf_op jit(solution)/shard_map/cy,xy->cx/dot_general | solution.py:167
  160.3 1.8 fusion.260
  162.1 1.8 fusion.259
  163.9 1.8 fusion.258
  165.6 1.9 fusion.217
  169.9 2.0 reshape.4840
  171.9 2.6 fusion.173
  175.6 3.3 reshape.4930
  179.0 6.0 %fusion.131 = f32[3,64,128]{2,0,1:T(4,128)S(1)} fusion(f32[64,3,21,21]{3,2,1,0:T(8,128)} %reshape.4930, f32[21,64,128]{2,0,1:T(8,128)} %copy.323, f32[21,64,128,1]{2,1,0,3:T(8,128)S(1)} %bitcast.1390), kind=kOutput, calls=%fused_computation.240 | convolution fusion | flops 131063808 | bytes 1813248 | tf_op jit(solution)/shard_map/ncjk,knp->cjnp/dot_general | solution.py:60
  186.3 29.1 %fusion.69 = (f32[64,128]{1,0:T(8,128)S(1)}, f32[64,128]{1,0:T(8,128)S(1)}, f32[64,128]{1,0:T(8,128)S(1)}, f32[64,128]{1,0:T(8,128)S(1)}, f32[64,128]{1,0:T(8,12...) fusion(f32[64,128]{1,0:T(8,128)S(1)} %get-tuple-element.142, ...), kind=kLoop, calls=%fused_computation.174 | loop fusion | flops 81715200 | bytes 884736 | tf_op jit(solution)/shard_map/while/body/eval_jaxpr/reduce_sum | solution.py:73
  219.6 5.5 %fusion.132 = f32[64,3,21,21]{3,2,1,0:T(8,128)} fusion(f32[21,64,128]{2,0,1:T(8,128)S(1)} %copy.364, f32[3,64,128]{2,0,1:T(4,128)S(1)} %copy-done.14, f32[21,64,128,1]{2,1,0,3:T(8,128)S(1)} %bitcast.1387), kind=kOutput, calls=%fused_computation.241 | convolution fusion | flops 130572288 | bytes 1813248 | tf_op jit(solution)/shard_map/cjnp,knp->ncjk/dot_general | solution.py:55
  225.2 3.3 copy.366
  228.4 1.4 add_convert_fusion
  229.9 1.7 copy.367
  232.4 1.6 fusion.448
  234.7 2.0 collective-permute-start.12
  237.3 2.1 convert_element_type.264
  241.6 1.4 convolution_convert_fusion
  243.0 1.7 reshape.4845
  244.7 2.6 copy.381
  248.6 3.0 collective-permute-start.9
  252.0 1.6 collective-permute-start.14
  253.7 1.9 collective-permute-done.14
  256.0 2.4 collective-permute-start.15
  258.4 2.1 collective-permute-done.15
  260.8 4.5 %collective-permute-start.16 = (bf16[3,441]{1,0:T(4,128)(2,1)S(1)}, bf16[3,441]{1,0:T(4,128)(2,1)S(1)}, u32[]{:S(2)}, u32[]{:S(2)}) collective-permute-start(bf16[3,441]{1,0:T(4,128)(2,1)S(1)} %fusion.249), channel_id=1, source_target_pairs={{0,8},{8,0},{1,9},{9,1},{2,10},{10,2},{3,11},{11,3},{4,12},{12,4},... | collective-permute-start | bytes 7946 | tf_op jit(solution)/shard_map/ppermute | solution.py:37
  265.3 24.4 %fusion.105 = (f32[64,128]{1,0:T(8,128)S(1)}, f32[64,128]{1,0:T(8,128)S(1)}, f32[64,128]{1,0:T(8,128)S(1)}, f32[64,128]{1,0:T(8,128)S(1)}, f32[64,128]{1,0:T(8,128)S(1)}, /*index=5*/f32[64,128]{1,0:T(8,128)}) fusion(f32[64,128]{1,0:T(8,128)S(1)} %get-tuple-element.154, f32[64,128]{1,0:T(8,128)S(1)} %get-tuple-element.155, ...), kind=kLoop, calls=%fused_computation.210 | loop fusion | flops 54476800 | bytes 688128 | tf_op jit(solution)/shard_map/while/body/eval_jaxpr/reduce_sum | solution.py:73
  290.0 25.9 %all-gather.3 = bf16[16,3,441]{2,1,0:T(4,128)(2,1)S(1)} all-gather(bf16[1,3,441]{2,1,0:T(4,128)(2,1)S(1)} %fusion.264), channel_id=3, replica_groups=mesh['sector'=16,'box'=16] {'sector'}, dimensions={0}, use_global_device_ids=true | all-gather | bytes 44982 | tf_op jit(solution)/shard_map/all_gather | solution.py:157
  315.9 4.6 %fusion.261 = f32[3,441]{1,0:T(4,128)S(1)} fusion(bf16[16,441,441]{2,1,0:T(8,128)(2,1)} %gather_fusion.3, bf16[1,441,441]{2,0,1:T(2,128)(2,1)} %get-tuple-element.125, bf16[16,3,441]{2,1,0:T(4,128)(2,1)S(1)} %all-gather.3, pred[16]{0:T(512)(128)(4,1)S(1)} %copy-done.61), kind=kOutput, calls=%fused_computation.343 | convolution fusion | flops 19859554 | bytes 6659998 | tf_op jit(solution)/shard_map/cy,xy->cx/dot_general | solution.py:167
  320.6 1.8 fusion.257
  322.4 1.8 fusion.256
  324.2 1.5 fusion.255
  325.7 1.9 fusion.218
  329.3 2.7 fusion.170
  333.1 2.5 reshape.4932
  335.7 5.2 %fusion.130 = f32[3,64,128]{2,0,1:T(4,128)S(1)} fusion(f32[64,3,21,21]{3,2,1,0:T(8,128)S(1)} %reshape.4932, f32[21,64,128]{2,0,1:T(8,128)S(1)} %copy-done.5, f32[21,64,128,1]{2,1,0,3:T(8,128)} %bitcast.1388), kind=kOutput, calls=%fused_computation.238 | convolution fusion | flops 131063808 | bytes 1813248 | tf_op jit(solution)/shard_map/ncjk,knp->cjnp/dot_general | solution.py:60
  342.1 28.9 %fusion.129 = (f32[64,128]{1,0:T(8,128)S(1)}, f32[64,128]{1,0:T(8,128)S(1)}, f32[64,128]{1,0:T(8,128)S(1)}, f32[64,128]{1,0:T(8,128)S(1)}, f32[64,128]{1,0:T(8,1...) fusion(f32[64,128]{1,0:T(8,128)S(1)} %get-tuple-element.130, ...), kind=kLoop, calls=%fused_computation.234 | loop fusion | flops 81715200 | bytes 884736 | tf_op jit(solution)/shard_map/while/body/eval_jaxpr/reduce_sum | solution.py:73
  (345 shorter events, 47.3 us)
Async XLA Ops:
  0.6 11.9 %copy-start.1 = (f32[3,1,64,128]{3,2,1,0:T(8,128)S(1)}, f32[3,1,64,128]{3,2,1,0:T(8,128)}, u32[]{:S(2)}) copy-start(f32[3,1,64,128]{3,2,1,0:T(8,128)} %param.12) | copy-start | bytes 294916
  0.6 11.8 %copy-start.60 = (s32[1,64]{1,0:T(1,128)S(1)}, s32[1,64]{1,0:T(1,128)}, u32[]{:S(2)}) copy-start(s32[1,64]{1,0:T(1,128)} %param.14) | copy-start | bytes 772
  3.0 9.5 %copy-start.21 = (bf16[3,1,64,128]{3,2,1,0:T(8,128)(2,1)}, bf16[3,1,64,128]{3,2,1,0:T(8,128)(2,1)S(1)}, u32[]{:S(2)}) copy-start(bf16[3,1,64,128]{3,2,1,0:T(8,128)(2,1)S(1)} %get-tuple-element.194) | copy-start | bytes 147460
  6.7 178.3 %collective-permute-start.3 = (bf16[6,1,64,128]{3,2,1,0:T(8,128)(2,1)}, bf16[6,1,64,128]{3,2,1,0:T(8,128)(2,1)}, u32[]{:S(2)}, u32[]{:S(2)}) collective-permute-start(bf16[6,1,64,128]{3,2,1,0:T(8,128)(2,1)} %get-tuple-element.196), channel_id=1, source_target_pairs={{16,0},{32,16},{48,32},{64,48},{80,64},{96,80},{112,96},{128,112},... | collective-permute-start | bytes 294920 | tf_op jit(solution)/shard_map/ppermute | solution.py:25
  9.0 176.0 %collective-permute-start.2 = (bf16[6,1,64,128]{3,2,1,0:T(8,128)(2,1)}, bf16[6,1,64,128]{3,2,1,0:T(8,128)(2,1)}, u32[]{:S(2)}, u32[]{:S(2)}) collective-permute-start(bf16[6,1,64,128]{3,2,1,0:T(8,128)(2,1)} %get-tuple-element.196), channel_id=1, source_target_pairs={{0,16},{16,32},{32,48},{48,64},{64,80},{80,96},{96,112},{112,128},... | collective-permute-start | bytes 294920 | tf_op jit(solution)/shard_map/ppermute | solution.py:24
  12.4 18.7 %copy-start.17 = (f32[3,1,64,128]{3,2,1,0:T(8,128)S(1)}, f32[3,1,64,128]{3,2,1,0:T(8,128)}, u32[]{:S(2)}) copy-start(f32[3,1,64,128]{3,2,1,0:T(8,128)} %param.13) | copy-start | bytes 294916
  15.2 21.2 %copy-start.2 = (bf16[2,441,441]{2,0,1:T(2,128)(2,1)S(1)}, bf16[2,441,441]{2,0,1:T(2,128)(2,1)}, u32[]{:S(2)}) copy-start(bf16[2,441,441]{2,0,1:T(2,128)(2,1)} %param.21) | copy-start | bytes 2333776
  23.1 42.2 %collective-permute-start.4 = (f32[6,256]{1,0:T(8,128)S(1)}, f32[6,256]{1,0:T(8,128)S(1)}, u32[]{:S(2)}, u32[]{:S(2)}) collective-permute-start(f32[6,256]{1,0:T(8,128)S(1)} %pad_maximum_fusion.6), channel_id=1, source_target_pairs={{0,16},{16,32},{32,48},{48,64},{64,80},{80,96},{96,112},{112,128},... | collective-permute-start | bytes 18440 | tf_op jit(solution)/shard_map/ppermute | solution.py:42
  25.0 57.4 %collective-permute-start.1 = (bf16[6,1,1,128]{3,2,0,1:T(2,128)(2,1)}, bf16[6,1,1,128]{3,2,0,1:T(2,128)(2,1)}, u32[]{:S(2)}, u32[]{:S(2)}) collective-permute-start(bf16[6,1,1,128]{3,2,0,1:T(2,128)(2,1)} %get-tuple-element.192), channel_id=1, source_target_pairs={{1,0},{2,1},{3,2},{4,3},{5,4},{6,5},{7,6},{8,7},{9,8},{10,9},{11,1... | collective-permute-start | bytes 4616 | tf_op jit(solution)/shard_map/ppermute | solution.py:25
  26.3 56.1 %collective-permute-start = (bf16[6,1,1,128]{3,2,0,1:T(2,128)(2,1)}, bf16[6,1,1,128]{3,2,0,1:T(2,128)(2,1)}, u32[]{:S(2)}, u32[]{:S(2)}) collective-permute-start(bf16[6,1,1,128]{3,2,0,1:T(2,128)(2,1)} %get-tuple-element.191), channel_id=1, source_target_pairs={{0,1},{1,2},{2,3},{3,4},{4,5},{5,6},{6,7},{7,8},{8,9},{9,10},{10,1... | collective-permute-start | bytes 4616 | tf_op jit(solution)/shard_map/ppermute | solution.py:24
  33.7 9.2 %copy-start.8 = (f32[21,64,128]{2,1,0:T(8,128)}, f32[21,64,128]{2,1,0:T(8,128)S(1)}, u32[]{:S(2)}) copy-start(f32[21,64,128]{2,1,0:T(8,128)S(1)} %get-tuple-element.203) | copy-start | bytes 2064388
  67.9 10.7 %copy-start = (bf16[4,441,441]{2,0,1:T(4,128)(2,1)S(1)}, bf16[4,441,441]{2,0,1:T(4,128)(2,1)}, u32[]{:S(2)}) copy-start(bf16[4,441,441]{2,0,1:T(4,128)(2,1)} %param.19) | copy-start | bytes 4667548
  81.4 1.8 collective-permute-start.5
  83.6 3.6 collective-permute-start.6
  87.5 30.8 %collective-permute-start.7 = (bf16[3,441]{1,0:T(4,128)(2,1)S(1)}, bf16[3,441]{1,0:T(4,128)(2,1)S(1)}, u32[]{:S(2)}, u32[]{:S(2)}) collective-permute-start(bf16[3,441]{1,0:T(4,128)(2,1)S(1)} %fusion.240), channel_id=1, source_target_pairs={{0,4},{4,0},{1,5},{5,1},{2,6},{6,2},{3,7},{7,3},{8,12},{12,8},{9,1... | collective-permute-start | bytes 7946 | tf_op jit(solution)/shard_map/ppermute | solution.py:37
  119.2 9.1 %collective-permute-start.8 = (bf16[3,441]{1,0:T(4,128)(2,1)}, bf16[3,441]{1,0:T(4,128)(2,1)}, u32[]{:S(2)}, u32[]{:S(2)}) collective-permute-start(bf16[3,441]{1,0:T(4,128)(2,1)} %fusion.241), channel_id=1, source_target_pairs={{0,8},{8,0},{1,9},{9,1},{2,10},{10,2},{3,11},{11,3},{4,12},{12,4},... | collective-permute-start | bytes 7946 | tf_op jit(solution)/shard_map/ppermute | solution.py:37
  169.9 9.0 %copy-start.9 = (f32[21,64,128]{2,1,0:T(8,128)S(1)}, f32[21,64,128]{2,1,0:T(8,128)}, u32[]{:S(2)}) copy-start(f32[21,64,128]{2,1,0:T(8,128)} %copy-done.8) | copy-start | bytes 2064388
  178.9 7.3 %copy-start.42 = (f32[64,128]{1,0:T(8,128)S(1)}, f32[64,128]{1,0:T(8,128)}, u32[]{:S(2)}) copy-start(f32[64,128]{1,0:T(8,128)} %get-tuple-element.197) | copy-start | bytes 98308
  178.9 7.3 %copy-start.44 = (f32[64,128]{1,0:T(8,128)S(1)}, f32[64,128]{1,0:T(8,128)}, u32[]{:S(2)}) copy-start(f32[64,128]{1,0:T(8,128)} %get-tuple-element.198) | copy-start | bytes 98308
  178.9 7.3 %copy-start.46 = (f32[64,128]{1,0:T(8,128)S(1)}, f32[64,128]{1,0:T(8,128)}, u32[]{:S(2)}) copy-start(f32[64,128]{1,0:T(8,128)} %get-tuple-element.199) | copy-start | bytes 98308
  178.9 7.3 %copy-start.48 = (f32[64,128]{1,0:T(8,128)S(1)}, f32[64,128]{1,0:T(8,128)}, u32[]{:S(2)}) copy-start(f32[64,128]{1,0:T(8,128)} %get-tuple-element.200) | copy-start | bytes 98308
  179.0 7.3 %copy-start.49 = (f32[64,128]{1,0:T(8,128)S(1)}, f32[64,128]{1,0:T(8,128)}, u32[]{:S(2)}) copy-start(f32[64,128]{1,0:T(8,128)} %get-tuple-element.201) | copy-start | bytes 98308
  179.0 7.3 %copy-start.50 = (f32[64,128]{1,0:T(8,128)S(1)}, f32[64,128]{1,0:T(8,128)}, u32[]{:S(2)}) copy-start(f32[64,128]{1,0:T(8,128)} %get-tuple-element.202) | copy-start | bytes 98308
  184.9 31.4 %copy-start.15 = (f32[3,64,128]{2,0,1:T(4,128)}, f32[3,64,128]{2,0,1:T(4,128)S(1)}, u32[]{:S(2)}) copy-start(f32[3,64,128]{2,0,1:T(4,128)S(1)} %fusion.131) | copy-start | bytes 294916
  184.9 30.6 %copy-start.26 = (f32[64,128]{1,0:T(8,128)S(1)}, f32[64,128]{1,0:T(8,128)}, u32[]{:S(2)}) copy-start(f32[64,128]{1,0:T(8,128)} %get-tuple-element.80) | copy-start | bytes 98308
  185.0 30.6 %copy-start.27 = (f32[64,128]{1,0:T(8,128)S(1)}, f32[64,128]{1,0:T(8,128)}, u32[]{:S(2)}) copy-start(f32[64,128]{1,0:T(8,128)} %get-tuple-element.81) | copy-start | bytes 98308
  185.0 30.6 %copy-start.28 = (f32[64,128]{1,0:T(8,128)S(1)}, f32[64,128]{1,0:T(8,128)}, u32[]{:S(2)}) copy-start(f32[64,128]{1,0:T(8,128)} %get-tuple-element.82) | copy-start | bytes 98308
  185.0 30.6 %copy-start.29 = (f32[64,128]{1,0:T(8,128)S(1)}, f32[64,128]{1,0:T(8,128)}, u32[]{:S(2)}) copy-start(f32[64,128]{1,0:T(8,128)} %get-tuple-element.107) | copy-start | bytes 98308
  185.0 30.6 %copy-start.30 = (f32[64,128]{1,0:T(8,128)S(1)}, f32[64,128]{1,0:T(8,128)}, u32[]{:S(2)}) copy-start(f32[64,128]{1,0:T(8,128)} %get-tuple-element.108) | copy-start | bytes 98308
  185.0 30.6 %copy-start.31 = (f32[64,128]{1,0:T(8,128)S(1)}, f32[64,128]{1,0:T(8,128)}, u32[]{:S(2)}) copy-start(f32[64,128]{1,0:T(8,128)} %get-tuple-element.109) | copy-start | bytes 98308
  185.0 31.3 %copy-start.6 = (f32[21,64,128]{2,1,0:T(8,128)S(1)}, f32[21,64,128]{2,1,0:T(8,128)}, u32[]{:S(2)}) copy-start(f32[21,64,128]{2,1,0:T(8,128)} %get-tuple-element.217) | copy-start | bytes 2064388
  185.0 31.3 %copy-start.20 = (f32[21,64,128]{2,1,0:T(8,128)S(1)}, f32[21,64,128]{2,1,0:T(8,128)}, u32[]{:S(2)}) copy-start(f32[21,64,128]{2,1,0:T(8,128)} %get-tuple-element.218) | copy-start | bytes 2064388
  186.3 33.3 %copy-start.14 = (f32[3,64,128]{2,0,1:T(4,128)S(1)}, f32[3,64,128]{2,0,1:T(4,128)}, u32[]{:S(2)}) copy-start(f32[3,64,128]{2,0,1:T(4,128)} %copy.322) | copy-start | bytes 294916
  215.5 9.6 %copy-start.32 = (f32[64,128]{1,0:T(8,128)}, f32[64,128]{1,0:T(8,128)S(1)}, u32[]{:S(2)}) copy-start(f32[64,128]{1,0:T(8,128)S(1)} %get-tuple-element.74) | copy-start | bytes 98308
  215.5 9.6 %copy-start.33 = (f32[64,128]{1,0:T(8,128)}, f32[64,128]{1,0:T(8,128)S(1)}, u32[]{:S(2)}) copy-start(f32[64,128]{1,0:T(8,128)S(1)} %get-tuple-element.75) | copy-start | bytes 98308
  215.5 9.6 %copy-start.34 = (f32[64,128]{1,0:T(8,128)}, f32[64,128]{1,0:T(8,128)S(1)}, u32[]{:S(2)}) copy-start(f32[64,128]{1,0:T(8,128)S(1)} %get-tuple-element.76) | copy-start | bytes 98308
  215.5 9.6 %copy-start.35 = (f32[64,128]{1,0:T(8,128)}, f32[64,128]{1,0:T(8,128)S(1)}, u32[]{:S(2)}) copy-start(f32[64,128]{1,0:T(8,128)S(1)} %get-tuple-element.101) | copy-start | bytes 98308
  215.5 9.6 %copy-start.36 = (f32[64,128]{1,0:T(8,128)}, f32[64,128]{1,0:T(8,128)S(1)}, u32[]{:S(2)}) copy-start(f32[64,128]{1,0:T(8,128)S(1)} %get-tuple-element.102) | copy-start | bytes 98308
  215.5 9.6 %copy-start.37 = (f32[64,128]{1,0:T(8,128)}, f32[64,128]{1,0:T(8,128)S(1)}, u32[]{:S(2)}) copy-start(f32[64,128]{1,0:T(8,128)S(1)} %get-tuple-element.103) | copy-start | bytes 98308
  215.5 9.6 %copy-start.38 = (f32[64,128]{1,0:T(8,128)}, f32[64,128]{1,0:T(8,128)S(1)}, u32[]{:S(2)}) copy-start(f32[64,128]{1,0:T(8,128)S(1)} %get-tuple-element.104) | copy-start | bytes 98308
  215.5 9.6 %copy-start.39 = (f32[64,128]{1,0:T(8,128)}, f32[64,128]{1,0:T(8,128)S(1)}, u32[]{:S(2)}) copy-start(f32[64,128]{1,0:T(8,128)S(1)} %get-tuple-element.105) | copy-start | bytes 98308
  215.5 9.6 %copy-start.40 = (f32[64,128]{1,0:T(8,128)}, f32[64,128]{1,0:T(8,128)S(1)}, u32[]{:S(2)}) copy-start(f32[64,128]{1,0:T(8,128)S(1)} %get-tuple-element.106) | copy-start | bytes 98308
  225.1 7.3 %copy-start.16 = (f32[3,64,128]{2,0,1:T(4,128)S(1)}, f32[3,64,128]{2,0,1:T(4,128)}, u32[]{:S(2)}) copy-start(f32[3,64,128]{2,0,1:T(4,128)} %copy-done.15) | copy-start | bytes 294916
  225.1 8.9 %copy-start.12 = (bf16[3,1,64,128]{3,2,1,0:T(8,128)(2,1)S(1)}, bf16[3,1,64,128]{3,2,1,0:T(8,128)(2,1)}, u32[]{:S(2)}) copy-start(bf16[3,1,64,128]{3,2,1,0:T(8,128)(2,1)} %copy-done.11) | copy-start | bytes 147460
  234.0 7.4 %copy-start.18 = (bf16[3,1,64,128]{3,2,1,0:T(8,128)(2,1)}, bf16[3,1,64,128]{3,2,1,0:T(8,128)(2,1)S(1)}, u32[]{:S(2)}) copy-start(bf16[3,1,64,128]{3,2,1,0:T(8,128)(2,1)S(1)} %get-tuple-element.114) | copy-start | bytes 147460
  234.7 106.2 %collective-permute-start.12 = (bf16[6,1,64,128]{3,2,1,0:T(8,128)(2,1)}, bf16[6,1,64,128]{3,2,1,0:T(8,128)(2,1)}, u32[]{:S(2)}, u32[]{:S(2)}) collective-permute-start(bf16[6,1,64,128]{3,2,1,0:T(8,128)(2,1)} %pad_maximum_fusion.2), channel_id=1, source_target_pairs={{16,0},{32,16},{48,32},{64,48},{80,64},{96,80},{112,96},{128,112},... | collective-permute-start | bytes 294920 | tf_op jit(solution)/shard_map/ppermute | solution.py:25
  236.7 104.2 %collective-permute-start.11 = (bf16[6,1,64,128]{3,2,1,0:T(8,128)(2,1)}, bf16[6,1,64,128]{3,2,1,0:T(8,128)(2,1)}, u32[]{:S(2)}, u32[]{:S(2)}) collective-permute-start(bf16[6,1,64,128]{3,2,1,0:T(8,128)(2,1)} %pad_maximum_fusion.2), channel_id=1, source_target_pairs={{0,16},{16,32},{32,48},{48,64},{64,80},{80,96},{96,112},{112,128},... | collective-permute-start | bytes 294920 | tf_op jit(solution)/shard_map/ppermute | solution.py:24
  240.2 8.4 %copy-start.22 = (bf16[3,64,128]{2,1,0:T(8,128)(2,1)S(1)}, bf16[3,64,128]{2,1,0:T(8,128)(2,1)}, u32[]{:S(2)}) copy-start(bf16[3,64,128]{2,1,0:T(8,128)(2,1)} %get-tuple-element.116) | copy-start | bytes 147460
  240.2 8.4 %copy-start.25 = (bf16[3,64,128]{2,1,0:T(8,128)(2,1)S(1)}, bf16[3,64,128]{2,1,0:T(8,128)(2,1)}, u32[]{:S(2)}) copy-start(bf16[3,64,128]{2,1,0:T(8,128)(2,1)} %get-tuple-element.112) | copy-start | bytes 147460
  241.4 10.3 %collective-permute-start.13 = (bf16[3,441]{1,0:T(4,128)(2,1)S(1)}, bf16[3,441]{1,0:T(4,128)(2,1)S(1)}, u32[]{:S(2)}, u32[]{:S(2)}) collective-permute-start(bf16[3,441]{1,0:T(4,128)(2,1)S(1)} %fusion.236), channel_id=1, source_target_pairs={{0,1},{1,0},{2,3},{3,2},{4,5},{5,4},{6,7},{7,6},{8,9},{9,8},{10,11... | collective-permute-start | bytes 7946 | tf_op jit(solution)/shard_map/ppermute | solution.py:37
  244.7 20.7 %copy-start.51 = (f32[64,128]{1,0:T(8,128)S(1)}, f32[64,128]{1,0:T(8,128)}, u32[]{:S(2)}) copy-start(f32[64,128]{1,0:T(8,128)} %get-tuple-element.180) | copy-start | bytes 98308
  244.7 20.7 %copy-start.53 = (f32[64,128]{1,0:T(8,128)S(1)}, f32[64,128]{1,0:T(8,128)}, u32[]{:S(2)}) copy-start(f32[64,128]{1,0:T(8,128)} %get-tuple-element.183) | copy-start | bytes 98308
  244.7 20.7 %copy-start.55 = (f32[64,128]{1,0:T(8,128)S(1)}, f32[64,128]{1,0:T(8,128)}, u32[]{:S(2)}) copy-start(f32[64,128]{1,0:T(8,128)} %get-tuple-element.184) | copy-start | bytes 98308
  247.3 6.4 %collective-permute-start.10 = (bf16[6,1,1,128]{3,2,1,0:T(2,128)(2,1)}, bf16[6,1,1,128]{3,2,1,0:T(2,128)(2,1)S(1)}, u32[]{:S(2)}, u32[]{:S(2)}) collective-permute-start(bf16[6,1,1,128]{3,2,1,0:T(2,128)(2,1)} %get-tuple-element.179), channel_id=1, source_target_pairs={{1,0},{2,1},{3,2},{4,3},{5,4},{6,5},{7,6},{8,7},{9,8},{10,9},{11,1... | collective-permute-start | bytes 4616 | tf_op jit(solution)/shard_map/ppermute | solution.py:25
  248.6 5.0 %collective-permute-start.9 = (bf16[6,1,1,128]{3,2,1,0:T(2,128)(2,1)S(1)}, bf16[6,1,1,128]{3,2,1,0:T(2,128)(2,1)S(1)}, u32[]{:S(2)}, u32[]{:S(2)}) collective-permute-start(bf16[6,1,1,128]{3,2,1,0:T(2,128)(2,1)S(1)} %get-tuple-element.178), channel_id=1, source_target_pairs={{0,1},{1,2},{2,3},{3,4},{4,5},{5,6},{6,7},{7,8},{8,9},{9,10},{10,1... | collective-permute-start | bytes 4616 | tf_op jit(solution)/shard_map/ppermute | solution.py:24
  251.8 64.1 %copy-start.61 = (pred[16]{0:T(512)(128)(4,1)S(1)}, pred[16]{0:T(512)(128)(4,1)}, u32[]{:S(2)}) copy-start(pred[16]{0:T(512)(128)(4,1)} %fusion.434) | copy-start | bytes 52
  252.0 3.6 collective-permute-start.14
  256.0 4.5 %collective-permute-start.15 = (bf16[3,441]{1,0:T(4,128)(2,1)S(1)}, bf16[3,441]{1,0:T(4,128)(2,1)S(1)}, u32[]{:S(2)}, u32[]{:S(2)}) collective-permute-start(bf16[3,441]{1,0:T(4,128)(2,1)S(1)} %fusion.248), channel_id=1, source_target_pairs={{0,4},{4,0},{1,5},{5,1},{2,6},{6,2},{3,7},{7,3},{8,12},{12,8},{9,1... | collective-permute-start | bytes 7946 | tf_op jit(solution)/shard_map/ppermute | solution.py:37
  260.8 28.9 %collective-permute-start.16 = (bf16[3,441]{1,0:T(4,128)(2,1)S(1)}, bf16[3,441]{1,0:T(4,128)(2,1)S(1)}, u32[]{:S(2)}, u32[]{:S(2)}) collective-permute-start(bf16[3,441]{1,0:T(4,128)(2,1)S(1)} %fusion.249), channel_id=1, source_target_pairs={{0,8},{8,0},{1,9},{9,1},{2,10},{10,2},{3,11},{11,3},{4,12},{12,4},... | collective-permute-start | bytes 7946 | tf_op jit(solution)/shard_map/ppermute | solution.py:37
  315.9 8.2 %copy-start.10 = (bf16[1,441,441]{2,0,1:T(2,128)(2,1)S(1)}, bf16[1,441,441]{2,0,1:T(2,128)(2,1)}, u32[]{:S(2)}) copy-start(bf16[1,441,441]{2,0,1:T(2,128)(2,1)} %get-tuple-element.122) | copy-start | bytes 1166890
  332.0 8.9 %copy-start.13 = (bf16[3,1,64,128]{3,2,1,0:T(8,128)(2,1)S(1)}, bf16[3,1,64,128]{3,2,1,0:T(8,128)(2,1)}, u32[]{:S(2)}) copy-start(bf16[3,1,64,128]{3,2,1,0:T(8,128)(2,1)} %copy-done.11) | copy-start | bytes 147460
  332.0 8.9 %copy-start.19 = (bf16[3,1,64,128]{3,2,1,0:T(8,128)(2,1)S(1)}, bf16[3,1,64,128]{3,2,1,0:T(8,128)(2,1)}, u32[]{:S(2)}) copy-start(bf16[3,1,64,128]{3,2,1,0:T(8,128)(2,1)} %copy-done.18) | copy-start | bytes 147460
  340.9 30.0 %copy-start.24 = (f32[3,1,64,128]{3,2,1,0:T(8,128)S(1)}, f32[3,1,64,128]{3,2,1,0:T(8,128)}, u32[]{:S(2)}) copy-start(f32[3,1,64,128]{3,2,1,0:T(8,128)} %get-tuple-element.115) | copy-start | bytes 294916
  340.9 30.0 %copy-start.41 = (f32[64,128]{1,0:T(8,128)S(1)}, f32[64,128]{1,0:T(8,128)}, u32[]{:S(2)}) copy-start(f32[64,128]{1,0:T(8,128)} %get-tuple-element.100) | copy-start | bytes 98308
  (16 other events, 86.9 us)
where the time goes:
time: 379 us; the launch traced here: 372 us
  other arithmetic  128 us (34%)
  local copies, waits for them, and re-layouts  80.1 us (21%)
  matrix products  69.6 us (18%)
  blocking collectives  51.6 us (14%)
  starting transfers between devices  34.2 us (9%)
  waiting for transfers between devices  5.86 us (2%)
    reduce_sum x4, other arithmetic, pair_velocity(): jnp.sum(inverse * (weight_y * delta_z - weight_z * delta_y), axis=2)  108 us
    all_gather x2, blocking collectives, far_field(): piece = lax.all_gather(current[None], 'sector', axis=0, tiled=True)  51.6 us
    dot_general x8, matrix products, far_field(): jnp.einsum('cy,xy->cx', local, up_side, preferred_element_type=jnp.float32)  19.6 us
    ppermute x8, starting transfers between devices, partner_2(): return lax.ppermute(block, axis, route)  19.3 us
    dot_general x2, matrix products, evaluate(): jnp.einsum('ncjk,knp->cjnp', shaped, cheb_b, precision=HIGHEST_PRECISION)  11.1 us
    dot_general x2, matrix products, multipoles(): jnp.einsum('cjnp,knp->ncjk', weighted, cheb_b, precision=HIGHEST_PRECISION)  10.9 us
    convert_element_type x6, local copies, waits for them, and re-layouts, far_field(): leaf = (multipoles(cheb_a, cheb_b, weights) + arrival_terms).reshape(box_...  10 us
    reshape x4, local copies, waits for them, and re-layouts, far_field(): presum = presum.astype(jnp.bfloat16).reshape(NCLASS, box_count * 3, coef)  8.64 us
  transfers between devices with their start and end apart: 17, of which 4 were waited for; matrix products, arithmetic and copies ran while one was open for 52% of the time, Pallas kernels for 0%

commit v1 on v0

--- a/solution.py
+++ b/solution.py
@@ -154,7 +154,16 @@
         current = merge_pair(current, partner, side_bit, tree_up)
     sector_index = lax.axis_index("sector")
     sector_count = lax.axis_size("sector")
-    piece = lax.all_gather(current[None], "sector", axis=0, tiled=True)
+    own = current[None]
+    devices_2 = lax.axis_size("sector")
+    held, tiles = (own, [own])
+    for _ in range(devices_2 - 1):
+        held = lax.ppermute(
+            held, "sector", [(i_2, (i_2 + 1) % devices_2) for i_2 in range(devices_2)]
+        )
+        tiles.insert(0, held)
+    line = jnp.concatenate(tiles, axis=0)
+    piece = jnp.roll(line, (lax.axis_index("sector") + 1) * own.shape[0], axis=0)
     source_ids = jnp.arange(piece.shape[0], dtype=jnp.int32)
     distance = (source_ids - sector_index) % sector_count
     matrices = m2l_sector[jnp.maximum(distance - 1, 0)]

time: 379 us -> 518 us (1.37)
  the two profiles are of different devices: /device:TPU:2 before, /device:TPU:30 now
where the time goes in v1:
time: 518 us; the launch traced here: 509 us
  starting transfers between devices  152 us (29%)
  other arithmetic  127 us (25%)
  local copies, waits for them, and re-layouts  105 us (20%)
  matrix products  75.1 us (14%)
  waiting for transfers between devices  46.9 us (9%)
    ppermute x30, starting transfers between devices, far_field(): lax.ppermute(held, 'sector', [(i_2, (i_2 + 1) % devices_2) for i_2 in ran...  118 us
    reduce_sum x4, other arithmetic, pair_velocity(): jnp.sum(inverse * (weight_y * delta_z - weight_z * delta_y), axis=2)  109 us
    ppermute x30, waiting for transfers between devices, far_field(): lax.ppermute(held, 'sector', [(i_2, (i_2 + 1) % devices_2) for i_2 in ran...  28.6 us
    unnamed x186, local copies, waits for them, and re-layouts  27.1 us
    dot_general x8, matrix products, far_field(): jnp.einsum('cy,xy->cx', local, up_side, preferred_element_type=jnp.float32)  22.1 us
    ppermute x8, waiting for transfers between devices, partner_2(): return lax.ppermute(block, axis, route)  18.3 us
    ppermute x4, starting transfers between devices, with_halo(): before = lax.ppermute(last, axis, up)  15.8 us
    ppermute x8, starting transfers between devices, partner_2(): return lax.ppermute(block, axis, route)  12.3 us
  transfers between devices with their start and end apart: 47, of which 26 were waited for; matrix products, arithmetic and copies ran while one was open for 38% of the time, Pallas kernels for 0%

profile of v1, /device:TPU:30, one launch (start us, length us, event | category | flops | bytes accessed | tf_op | source)
XLA Modules:
  0.0 508.8 jit_solution(11413444478604988614)
XLA Ops:
  1.4 3.4 copy.326
  4.9 2.9 gather_fusion.1
  9.7 2.7 copy.325
  12.4 2.9 gather_fusion
  20.8 5.4 %fusion.134 = f32[64,3,21,21]{3,2,1,0:T(8,128)} fusion(f32[21,64,128]{2,0,1:T(8,128)S(1)} %copy.323, f32[3,64,128]{2,0,1:T(4,128)S(1)} %copy.322, f32[21,64,128,1]{2,1,0,3:T(8,128)S(1)} %bitcast.1389), kind=kOutput, calls=%fused_computation.243 | convolution fusion | flops 130572288 | bytes 1813248 | tf_op jit(solution)/shard_map/cjnp,knp->ncjk/dot_general | solution.py:55
  26.2 6.4 %constant_dynamic-slice_fusion.1 = (bf16[1,441,441]{2,0,1:T(2,128)(2,1)}, bf16[1,441,441]{2,0,1:T(2,128)(2,1)}, bf16[1,441,441]{2,0,1:T(2,128)(2,1)}, bf16[1,441...) fusion(bf16[2,441,441]{2,0,1:T(2,128)(2,1)S(1)} %copy-done.2, s32[]{:T(128)S(6)} %select_n.171, ...), kind=kLoop, calls=%fused_computation.848 | loop fusion | bytes 4667560 | tf_op jit(solution)/shard_map/jit(dynamic_index_in_dim)/dynamic_slice | solution.py:174
  32.6 3.2 copy.329
  40.1 3.0 add_convert_fusion.1
  49.7 3.4 collective-permute-done.6
  55.0 3.0 collective-permute-done.7
  58.3 5.5 %collective-permute-start.8 = (bf16[3,441]{1,0:T(4,128)(2,1)S(1)}, bf16[3,441]{1,0:T(4,128)(2,1)S(1)}, u32[]{:S(2)}, u32[]{:S(2)}) collective-permute-start(bf16[3,441]{1,0:T(4,128)(2,1)S(1)} %fusion.241), channel_id=1, source_target_pairs={{0,8},{8,0},{1,9},{9,1},{2,10},{10,2},{3,11},{11,3},{4,12},{12,4},... | collective-permute-start | bytes 7946 | tf_op jit(solution)/shard_map/ppermute | solution.py:37
  66.3 3.8 collective-permute-start.2
  72.5 3.6 collective-permute-start
  78.4 6.7 %constant_dynamic-slice_fusion = (bf16[1,441,441]{2,0,1:T(2,128)(2,1)}, bf16[1,441,441]{2,0,1:T(2,128)(2,1)}, bf16[1,441,441]{2,0,1:T(2,128)(2,1)}, bf16[1,441,441]{2,0,1:T(2,128)(2,1)}) fusion(bf16[2,441,441]{2,0,1:T(2,128)(2,1)} %param.24, s32[]{:T(128)S(6)} %select_n.171, s32[]{:T(128)S(6)} %select_n.170, s32[]{:T(128)S(6)} %select_n.169, s32[]{:T(128)S(6)} %select_n.168), kind=kLoop, calls=%fused_computation.847 | loop fusion | bytes 3111712 | tf_op jit(solution)/shard_map/jit(dynamic_index_in_dim)/dynamic_slice | solution.py:175
  85.4 3.4 collective-permute-done.11
  88.8 3.5 collective-permute-start.12
  93.6 5.6 %collective-permute-start.13 = (bf16[1,3,441]{2,1,0:T(4,128)(2,1)S(1)}, bf16[1,3,441]{2,1,0:T(4,128)(2,1)S(1)}, u32[]{:S(2)}, u32[]{:S(2)}) collective-permute-start(bf16[1,3,441]{2,1,0:T(4,128)(2,1)S(1)} %collective-permute-done.12), channel_id=1, source_target_pairs={{0,16},{16,32},{32,48},{48,64},{64,80},{80,96},{96,112},{112,128},... | collective-permute-start | bytes 7946 | tf_op jit(solution)/shard_map/ppermute | solution.py:161
  100.6 5.6 %collective-permute-start.14 = (bf16[1,3,441]{2,1,0:T(4,128)(2,1)S(1)}, bf16[1,3,441]{2,1,0:T(4,128)(2,1)S(1)}, u32[]{:S(2)}, u32[]{:S(2)}) collective-permute-start(bf16[1,3,441]{2,1,0:T(4,128)(2,1)S(1)} %collective-permute-done.13), channel_id=1, source_target_pairs={{0,16},{16,32},{32,48},{48,64},{64,80},{80,96},{96,112},{112,128},... | collective-permute-start | bytes 7946 | tf_op jit(solution)/shard_map/ppermute | solution.py:161
  107.5 5.6 %collective-permute-start.15 = (bf16[1,3,441]{2,1,0:T(4,128)(2,1)S(1)}, bf16[1,3,441]{2,1,0:T(4,128)(2,1)S(1)}, u32[]{:S(2)}, u32[]{:S(2)}) collective-permute-start(bf16[1,3,441]{2,1,0:T(4,128)(2,1)S(1)} %collective-permute-done.14), channel_id=1, source_target_pairs={{0,16},{16,32},{32,48},{48,64},{64,80},{80,96},{96,112},{112,128},... | collective-permute-start | bytes 7946 | tf_op jit(solution)/shard_map/ppermute | solution.py:161
  114.5 5.7 %collective-permute-start.16 = (bf16[1,3,441]{2,1,0:T(4,128)(2,1)S(1)}, bf16[1,3,441]{2,1,0:T(4,128)(2,1)S(1)}, u32[]{:S(2)}, u32[]{:S(2)}) collective-permute-start(bf16[1,3,441]{2,1,0:T(4,128)(2,1)S(1)} %collective-permute-done.15), channel_id=1, source_target_pairs={{0,16},{16,32},{32,48},{48,64},{64,80},{80,96},{96,112},{112,128},... | collective-permute-start | bytes 7946 | tf_op jit(solution)/shard_map/ppermute | solution.py:161
  121.5 5.6 %collective-permute-start.17 = (bf16[1,3,441]{2,1,0:T(4,128)(2,1)S(1)}, bf16[1,3,441]{2,1,0:T(4,128)(2,1)S(1)}, u32[]{:S(2)}, u32[]{:S(2)}) collective-permute-start(bf16[1,3,441]{2,1,0:T(4,128)(2,1)S(1)} %collective-permute-done.16), channel_id=1, source_target_pairs={{0,16},{16,32},{32,48},{48,64},{64,80},{80,96},{96,112},{112,128},... | collective-permute-start | bytes 7946 | tf_op jit(solution)/shard_map/ppermute | solution.py:161
  128.4 5.6 %collective-permute-start.18 = (bf16[1,3,441]{2,1,0:T(4,128)(2,1)S(1)}, bf16[1,3,441]{2,1,0:T(4,128)(2,1)S(1)}, u32[]{:S(2)}, u32[]{:S(2)}) collective-permute-start(bf16[1,3,441]{2,1,0:T(4,128)(2,1)S(1)} %collective-permute-done.17), channel_id=1, source_target_pairs={{0,16},{16,32},{32,48},{48,64},{64,80},{80,96},{96,112},{112,128},... | collective-permute-start | bytes 7946 | tf_op jit(solution)/shard_map/ppermute | solution.py:161
  135.3 5.6 %collective-permute-start.19 = (bf16[1,3,441]{2,1,0:T(4,128)(2,1)S(1)}, bf16[1,3,441]{2,1,0:T(4,128)(2,1)S(1)}, u32[]{:S(2)}, u32[]{:S(2)}) collective-permute-start(bf16[1,3,441]{2,1,0:T(4,128)(2,1)S(1)} %collective-permute-done.18), channel_id=1, source_target_pairs={{0,16},{16,32},{32,48},{48,64},{64,80},{80,96},{96,112},{112,128},... | collective-permute-start | bytes 7946 | tf_op jit(solution)/shard_map/ppermute | solution.py:161
  141.5 6.9 %gather_fusion.3 = bf16[16,441,441]{2,1,0:T(8,128)(2,1)} fusion(bf16[15,441,441]{2,1,0:T(8,128)(2,1)} %param.25, s32[1024]{0:T(1024)S(1)} %pad_clamp_fusion), kind=kCustom, calls=%fused_computation.3 | custom fusion | bytes 12446848 | tf_op jit(solution)/shard_map/gather | solution.py:169
  149.6 2.6 collective-permute-done.20
  152.2 3.3 collective-permute-start.21
  156.9 5.7 %collective-permute-start.22 = (bf16[1,3,441]{2,1,0:T(4,128)(2,1)}, bf16[1,3,441]{2,1,0:T(4,128)(2,1)}, u32[]{:S(2)}, u32[]{:S(2)}) collective-permute-start(bf16[1,3,441]{2,1,0:T(4,128)(2,1)} %collective-permute-done.21), channel_id=1, source_target_pairs={{0,16},{16,32},{32,48},{48,64},{64,80},{80,96},{96,112},{112,128},... | collective-permute-start | bytes 7946 | tf_op jit(solution)/shard_map/ppermute | solution.py:161
  162.6 25.5 %fusion.45 = (f32[64,128]{1,0:T(8,128)S(1)}, f32[64,128]{1,0:T(8,128)}, f32[64,128]{1,0:T(8,128)}, f32[64,128]{1,0:T(8,128)}, f32[64,128]{1,0:T(8,128)}, /*index=5*/f32[64,128]{1,0:T(8,128)}) fusion(f32[64,128]{1,0:T(8,128)S(1)} %get-tuple-element.167, f32[64,128]{1,0:T(8,128)S(1)} %get-tuple-element.168, f32[64,128]{1,0:T(8,128)S(1)} %get-tuple-element.169, ...), kind=kLoop, calls=%fused_computation.150 | loop fusion | flops 54476800 | bytes 688128 | tf_op jit(solution)/shard_map/while/body/eval_jaxpr/reduce_sum | solution.py:73
  192.5 2.6 reshape.4841
  195.1 2.7 copy.356
  218.2 5.2 %fusion.262 = f32[3,441]{1,0:T(4,128)} fusion(bf16[16,441,441]{2,1,0:T(8,128)(2,1)} %gather_fusion.3, bf16[1,441,441]{2,0,1:T(2,128)(2,1)} %get-tuple-element.126, s32[]{:T(128)S(6)} %select_n.184, bf16[16,3,441]{2,1,0:T(4,128)(2,1)} %constant_dynamic-update-slice_fusion.84, pred[16]{0:T(512)(128)(4,1)} %fusion.442), kind=kOutput, calls=%fused_computation.344 | convolution fusion | flops 19944226 | bytes 6660002 | tf_op jit(solution)/shard_map/cy,xy->cx/dot_general | solution.py:176
  240.9 2.6 fusion.173
  244.6 3.5 reshape.4922
  248.2 6.1 %fusion.131 = f32[3,64,128]{2,0,1:T(4,128)S(1)} fusion(f32[64,3,21,21]{3,2,1,0:T(8,128)} %reshape.4922, f32[21,64,128]{2,0,1:T(8,128)} %copy-done.3, f32[21,64,128,1]{2,1,0,3:T(8,128)} %bitcast.1390), kind=kOutput, calls=%fused_computation.240 | convolution fusion | flops 131063808 | bytes 1813248 | tf_op jit(solution)/shard_map/ncjk,knp->cjnp/dot_general | solution.py:60
  255.6 29.3 %fusion.69 = (f32[64,128]{1,0:T(8,128)S(1)}, f32[64,128]{1,0:T(8,128)S(1)}, f32[64,128]{1,0:T(8,128)S(1)}, f32[64,128]{1,0:T(8,128)S(1)}, f32[64,128]{1,0:T(8,12...) fusion(f32[64,128]{1,0:T(8,128)S(1)} %get-tuple-element.143, ...), kind=kLoop, calls=%fused_computation.174 | loop fusion | flops 81715200 | bytes 884736 | tf_op jit(solution)/shard_map/while/body/eval_jaxpr/reduce_sum | solution.py:73
  289.0 5.5 %fusion.132 = f32[64,3,21,21]{3,2,1,0:T(8,128)} fusion(f32[21,64,128]{2,0,1:T(8,128)S(1)} %copy.364, f32[3,64,128]{2,0,1:T(4,128)S(1)} %copy-done.12, f32[21,64,128,1]{2,1,0,3:T(8,128)S(1)} %bitcast.1387), kind=kOutput, calls=%fused_computation.241 | convolution fusion | flops 130572288 | bytes 1813248 | tf_op jit(solution)/shard_map/cjnp,knp->ncjk/dot_general | solution.py:55
  294.5 3.2 copy.366
  299.9 2.7 copy.367
  302.6 2.8 convert_element_type.264
  312.2 2.6 collective-permute-done.29
  316.6 3.0 collective-permute-done.30
  320.0 2.5 collective-permute-start.31
  322.5 5.1 %collective-permute-done.31 = bf16[3,441]{1,0:T(4,128)(2,1)S(1)} collective-permute-done((bf16[3,441]{1,0:T(4,128)(2,1)S(1)}, bf16[3,441]{1,0:T(4,128)(2,1)S(1)}, u32[]{:S(2)}, u32[]{:S(2)}) %collective-permute-start.31) | collective-permute-done | bytes 2678 | tf_op jit(solution)/shard_map/ppermute | solution.py:37
  328.0 3.6 collective-permute-done.32
  331.6 3.3 collective-permute-start.33
  336.3 5.6 %collective-permute-start.34 = (bf16[1,3,441]{2,1,0:T(4,128)(2,1)S(1)}, bf16[1,3,441]{2,1,0:T(4,128)(2,1)S(1)}, u32[]{:S(2)}, u32[]{:S(2)}) collective-permute-start(bf16[1,3,441]{2,1,0:T(4,128)(2,1)S(1)} %collective-permute-done.33), channel_id=1, source_target_pairs={{0,16},{16,32},{32,48},{48,64},{64,80},{80,96},{96,112},{112,128},... | collective-permute-start | bytes 7946 | tf_op jit(solution)/shard_map/ppermute | solution.py:161
  343.2 5.6 %collective-permute-start.35 = (bf16[1,3,441]{2,1,0:T(4,128)(2,1)S(1)}, bf16[1,3,441]{2,1,0:T(4,128)(2,1)S(1)}, u32[]{:S(2)}, u32[]{:S(2)}) collective-permute-start(bf16[1,3,441]{2,1,0:T(4,128)(2,1)S(1)} %collective-permute-done.34), channel_id=1, source_target_pairs={{0,16},{16,32},{32,48},{48,64},{64,80},{80,96},{96,112},{112,128},... | collective-permute-start | bytes 7946 | tf_op jit(solution)/shard_map/ppermute | solution.py:161
  350.1 5.6 %collective-permute-start.36 = (bf16[1,3,441]{2,1,0:T(4,128)(2,1)S(1)}, bf16[1,3,441]{2,1,0:T(4,128)(2,1)S(1)}, u32[]{:S(2)}, u32[]{:S(2)}) collective-permute-start(bf16[1,3,441]{2,1,0:T(4,128)(2,1)S(1)} %collective-permute-done.35), channel_id=1, source_target_pairs={{0,16},{16,32},{32,48},{48,64},{64,80},{80,96},{96,112},{112,128},... | collective-permute-start | bytes 7946 | tf_op jit(solution)/shard_map/ppermute | solution.py:161
  357.1 5.6 %collective-permute-start.37 = (bf16[1,3,441]{2,1,0:T(4,128)(2,1)S(1)}, bf16[1,3,441]{2,1,0:T(4,128)(2,1)S(1)}, u32[]{:S(2)}, u32[]{:S(2)}) collective-permute-start(bf16[1,3,441]{2,1,0:T(4,128)(2,1)S(1)} %collective-permute-done.36), channel_id=1, source_target_pairs={{0,16},{16,32},{32,48},{48,64},{64,80},{80,96},{96,112},{112,128},... | collective-permute-start | bytes 7946 | tf_op jit(solution)/shard_map/ppermute | solution.py:161
  364.0 5.6 %collective-permute-start.38 = (bf16[1,3,441]{2,1,0:T(4,128)(2,1)S(1)}, bf16[1,3,441]{2,1,0:T(4,128)(2,1)S(1)}, u32[]{:S(2)}, u32[]{:S(2)}) collective-permute-start(bf16[1,3,441]{2,1,0:T(4,128)(2,1)S(1)} %collective-permute-done.37), channel_id=1, source_target_pairs={{0,16},{16,32},{32,48},{48,64},{64,80},{80,96},{96,112},{112,128},... | collective-permute-start | bytes 7946 | tf_op jit(solution)/shard_map/ppermute | solution.py:161
  370.9 5.6 %collective-permute-start.39 = (bf16[1,3,441]{2,1,0:T(4,128)(2,1)S(1)}, bf16[1,3,441]{2,1,0:T(4,128)(2,1)S(1)}, u32[]{:S(2)}, u32[]{:S(2)}) collective-permute-start(bf16[1,3,441]{2,1,0:T(4,128)(2,1)S(1)} %collective-permute-done.38), channel_id=1, source_target_pairs={{0,16},{16,32},{32,48},{48,64},{64,80},{80,96},{96,112},{112,128},... | collective-permute-start | bytes 7946 | tf_op jit(solution)/shard_map/ppermute | solution.py:161
  378.3 5.2 %collective-permute-start.40 = (bf16[1,3,441]{2,1,0:T(4,128)(2,1)S(1)}, bf16[1,3,441]{2,1,0:T(4,128)(2,1)S(1)}, u32[]{:S(2)}, u32[]{:S(2)}) collective-permute-start(bf16[1,3,441]{2,1,0:T(4,128)(2,1)S(1)} %collective-permute-done.39), channel_id=1, source_target_pairs={{0,16},{16,32},{32,48},{48,64},{64,80},{80,96},{96,112},{112,128},... | collective-permute-start | bytes 7946 | tf_op jit(solution)/shard_map/ppermute | solution.py:161
  385.3 5.3 %collective-permute-start.26 = (bf16[6,1,64,128]{3,2,1,0:T(8,128)(2,1)}, bf16[6,1,64,128]{3,2,1,0:T(8,128)(2,1)}, u32[]{:S(2)}, u32[]{:S(2)}) collective-permute-start(bf16[6,1,64,128]{3,2,1,0:T(8,128)(2,1)} %pad_maximum_fusion.2), channel_id=1, source_target_pairs={{0,16},{16,32},{32,48},{48,64},{64,80},{80,96},{96,112},{112,128},... | collective-permute-start | bytes 294920 | tf_op jit(solution)/shard_map/ppermute | solution.py:24
  394.3 4.6 collective-permute-start.42
  400.9 3.0 collective-permute-start.24
  410.4 2.6 collective-permute-start.44
  414.3 5.6 %collective-permute-start.45 = (bf16[1,3,441]{2,1,0:T(4,128)(2,1)S(1)}, bf16[1,3,441]{2,1,0:T(4,128)(2,1)S(1)}, u32[]{:S(2)}, u32[]{:S(2)}) collective-permute-start(bf16[1,3,441]{2,1,0:T(4,128)(2,1)S(1)} %collective-permute-done.44), channel_id=1, source_target_pairs={{0,16},{16,32},{32,48},{48,64},{64,80},{80,96},{96,112},{112,128},... | collective-permute-start | bytes 7946 | tf_op jit(solution)/shard_map/ppermute | solution.py:161
  421.2 5.6 %collective-permute-start.46 = (bf16[1,3,441]{2,1,0:T(4,128)(2,1)S(1)}, bf16[1,3,441]{2,1,0:T(4,128)(2,1)S(1)}, u32[]{:S(2)}, u32[]{:S(2)}) collective-permute-start(bf16[1,3,441]{2,1,0:T(4,128)(2,1)S(1)} %collective-permute-done.45), channel_id=1, source_target_pairs={{0,16},{16,32},{32,48},{48,64},{64,80},{80,96},{96,112},{112,128},... | collective-permute-start | bytes 7946 | tf_op jit(solution)/shard_map/ppermute | solution.py:161
  426.8 25.6 %fusion.105 = (f32[64,128]{1,0:T(8,128)}, f32[64,128]{1,0:T(8,128)}, f32[64,128]{1,0:T(8,128)}, f32[64,128]{1,0:T(8,128)}, f32[64,128]{1,0:T(8,128)}, /*index=5*/f32[64,128]{1,0:T(8,128)}) fusion(f32[64,128]{1,0:T(8,128)S(1)} %get-tuple-element.155, f32[64,128]{1,0:T(8,128)S(1)} %get-tuple-element.156, f32[64,128]{1,0:T(8,128)S(1)} %get-tuple-element.157, ...), kind=kLoop, calls=%fused_computation.210 | loop fusion | flops 54476800 | bytes 688128 | tf_op jit(solution)/shard_map/while/body/eval_jaxpr/reduce_sum | solution.py:73
  452.6 4.7 fusion.261
  466.0 2.7 fusion.170
  469.1 2.8 reshape.4924
  471.8 5.7 %fusion.130 = f32[3,64,128]{2,0,1:T(4,128)S(1)} fusion(f32[64,3,21,21]{3,2,1,0:T(8,128)} %reshape.4924, f32[21,64,128]{2,0,1:T(8,128)S(1)} %copy-done.5, f32[21,64,128,1]{2,1,0,3:T(8,128)S(1)} %bitcast.1388), kind=kOutput, calls=%fused_computation.238 | convolution fusion | flops 131063808 | bytes 1813248 | tf_op jit(solution)/shard_map/ncjk,knp->cjnp/dot_general | solution.py:60
  478.8 28.9 %fusion.129 = (f32[64,128]{1,0:T(8,128)S(1)}, f32[64,128]{1,0:T(8,128)S(1)}, f32[64,128]{1,0:T(8,128)S(1)}, f32[64,128]{1,0:T(8,128)S(1)}, f32[64,128]{1,0:T(8,1...) fusion(f32[64,128]{1,0:T(8,128)S(1)} %get-tuple-element.131, ...), kind=kLoop, calls=%fused_computation.234 | loop fusion | flops 81715200 | bytes 884736 | tf_op jit(solution)/shard_map/while/body/eval_jaxpr/reduce_sum | solution.py:73
  (457 shorter events, 137.5 us)
Async XLA Ops:
  15.4 20.5 %collective-permute-start.4 = (f32[6,256]{1,0:T(8,128)S(1)}, f32[6,256]{1,0:T(8,128)S(1)}, u32[]{:S(2)}, u32[]{:S(2)}) collective-permute-start(f32[6,256]{1,0:T(8,128)S(1)} %pad_maximum_fusion.6), channel_id=1, source_target_pairs={{0,16},{16,32},{32,48},{48,64},{64,80},{80,96},{96,112},{112,128},... | collective-permute-start | bytes 18440 | tf_op jit(solution)/shard_map/ppermute | solution.py:42
  20.7 43.1 %copy-start.8 = (bf16[3,1,64,128]{3,2,1,0:T(8,128)(2,1)}, bf16[3,1,64,128]{3,2,1,0:T(8,128)(2,1)S(1)}, u32[]{:S(2)}) copy-start(bf16[3,1,64,128]{3,2,1,0:T(8,128)(2,1)S(1)} %get-tuple-element.177) | copy-start | bytes 147460
  47.5 1.7 collective-permute-start.5
  49.5 3.6 collective-permute-start.6
  53.5 4.5 collective-permute-start.7
  58.3 11.9 %collective-permute-start.8 = (bf16[3,441]{1,0:T(4,128)(2,1)S(1)}, bf16[3,441]{1,0:T(4,128)(2,1)S(1)}, u32[]{:S(2)}, u32[]{:S(2)}) collective-permute-start(bf16[3,441]{1,0:T(4,128)(2,1)S(1)} %fusion.241), channel_id=1, source_target_pairs={{0,8},{8,0},{1,9},{9,1},{2,10},{10,2},{3,11},{11,3},{4,12},{12,4},... | collective-permute-start | bytes 7946 | tf_op jit(solution)/shard_map/ppermute | solution.py:37
  64.4 189.9 %collective-permute-start.3 = (bf16[6,1,64,128]{3,2,1,0:T(8,128)(2,1)}, bf16[6,1,64,128]{3,2,1,0:T(8,128)(2,1)}, u32[]{:S(2)}, u32[]{:S(2)}) collective-permute-start(bf16[6,1,64,128]{3,2,1,0:T(8,128)(2,1)} %get-tuple-element.197), channel_id=1, source_target_pairs={{16,0},{32,16},{48,32},{64,48},{80,64},{96,80},{112,96},{128,112},... | collective-permute-start | bytes 294920 | tf_op jit(solution)/shard_map/ppermute | solution.py:25
  66.3 188.1 %collective-permute-start.2 = (bf16[6,1,64,128]{3,2,1,0:T(8,128)(2,1)}, bf16[6,1,64,128]{3,2,1,0:T(8,128)(2,1)}, u32[]{:S(2)}, u32[]{:S(2)}) collective-permute-start(bf16[6,1,64,128]{3,2,1,0:T(8,128)(2,1)} %get-tuple-element.197), channel_id=1, source_target_pairs={{0,16},{16,32},{32,48},{48,64},{64,80},{80,96},{96,112},{112,128},... | collective-permute-start | bytes 294920 | tf_op jit(solution)/shard_map/ppermute | solution.py:24
  70.5 36.6 %copy-start.57 = (bf16[1,3,441]{2,1,0:T(4,128)(2,1)}, bf16[1,3,441]{2,1,0:T(4,128)(2,1)S(1)}, u32[]{:S(2)}) copy-start(bf16[1,3,441]{2,1,0:T(4,128)(2,1)S(1)} %fusion.266) | copy-start | bytes 7942
  70.5 5.6 %collective-permute-start.9 = (bf16[1,3,441]{2,1,0:T(4,128)(2,1)S(1)}, bf16[1,3,441]{2,1,0:T(4,128)(2,1)S(1)}, u32[]{:S(2)}, u32[]{:S(2)}) collective-permute-start(bf16[1,3,441]{2,1,0:T(4,128)(2,1)S(1)} %fusion.266), channel_id=1, source_target_pairs={{0,16},{16,32},{32,48},{48,64},{64,80},{80,96},{96,112},{112,128},... | collective-permute-start | bytes 7946 | tf_op jit(solution)/shard_map/ppermute | solution.py:161
  71.2 77.5 %collective-permute-start.1 = (bf16[6,1,1,128]{3,2,0,1:T(2,128)(2,1)}, bf16[6,1,1,128]{3,2,0,1:T(2,128)(2,1)}, u32[]{:S(2)}, u32[]{:S(2)}) collective-permute-start(bf16[6,1,1,128]{3,2,0,1:T(2,128)(2,1)} %get-tuple-element.193), channel_id=1, source_target_pairs={{1,0},{2,1},{3,2},{4,3},{5,4},{6,5},{7,6},{8,7},{9,8},{10,9},{11,1... | collective-permute-start | bytes 4616 | tf_op jit(solution)/shard_map/ppermute | solution.py:25
  72.5 76.2 %collective-permute-start = (bf16[6,1,1,128]{3,2,0,1:T(2,128)(2,1)}, bf16[6,1,1,128]{3,2,0,1:T(2,128)(2,1)}, u32[]{:S(2)}, u32[]{:S(2)}) collective-permute-start(bf16[6,1,1,128]{3,2,0,1:T(2,128)(2,1)} %get-tuple-element.192), channel_id=1, source_target_pairs={{0,1},{1,2},{2,3},{3,4},{4,5},{5,6},{6,7},{7,8},{8,9},{9,10},{10,1... | collective-permute-start | bytes 4616 | tf_op jit(solution)/shard_map/ppermute | solution.py:24
  76.1 31.0 %copy-start.60 = (bf16[1,3,441]{2,1,0:T(4,128)(2,1)}, bf16[1,3,441]{2,1,0:T(4,128)(2,1)S(1)}, u32[]{:S(2)}) copy-start(bf16[1,3,441]{2,1,0:T(4,128)(2,1)S(1)} %collective-permute-done.9) | copy-start | bytes 7942
  76.1 9.0 %collective-permute-start.10 = (bf16[1,3,441]{2,1,0:T(4,128)(2,1)S(1)}, bf16[1,3,441]{2,1,0:T(4,128)(2,1)S(1)}, u32[]{:S(2)}, u32[]{:S(2)}) collective-permute-start(bf16[1,3,441]{2,1,0:T(4,128)(2,1)S(1)} %collective-permute-done.9), channel_id=1, source_target_pairs={{0,16},{16,32},{32,48},{48,64},{64,80},{80,96},{96,112},{112,128},... | collective-permute-start | bytes 7946 | tf_op jit(solution)/shard_map/ppermute | solution.py:161
  85.1 3.7 collective-permute-start.11
  88.8 4.8 collective-permute-start.12
  93.6 6.9 %collective-permute-start.13 = (bf16[1,3,441]{2,1,0:T(4,128)(2,1)S(1)}, bf16[1,3,441]{2,1,0:T(4,128)(2,1)S(1)}, u32[]{:S(2)}, u32[]{:S(2)}) collective-permute-start(bf16[1,3,441]{2,1,0:T(4,128)(2,1)S(1)} %collective-permute-done.12), channel_id=1, source_target_pairs={{0,16},{16,32},{32,48},{48,64},{64,80},{80,96},{96,112},{112,128},... | collective-permute-start | bytes 7946 | tf_op jit(solution)/shard_map/ppermute | solution.py:161
  100.6 6.9 %collective-permute-start.14 = (bf16[1,3,441]{2,1,0:T(4,128)(2,1)S(1)}, bf16[1,3,441]{2,1,0:T(4,128)(2,1)S(1)}, u32[]{:S(2)}, u32[]{:S(2)}) collective-permute-start(bf16[1,3,441]{2,1,0:T(4,128)(2,1)S(1)} %collective-permute-done.13), channel_id=1, source_target_pairs={{0,16},{16,32},{32,48},{48,64},{64,80},{80,96},{96,112},{112,128},... | collective-permute-start | bytes 7946 | tf_op jit(solution)/shard_map/ppermute | solution.py:161
  107.5 6.9 %collective-permute-start.15 = (bf16[1,3,441]{2,1,0:T(4,128)(2,1)S(1)}, bf16[1,3,441]{2,1,0:T(4,128)(2,1)S(1)}, u32[]{:S(2)}, u32[]{:S(2)}) collective-permute-start(bf16[1,3,441]{2,1,0:T(4,128)(2,1)S(1)} %collective-permute-done.14), channel_id=1, source_target_pairs={{0,16},{16,32},{32,48},{48,64},{64,80},{80,96},{96,112},{112,128},... | collective-permute-start | bytes 7946 | tf_op jit(solution)/shard_map/ppermute | solution.py:161
  114.5 7.0 %collective-permute-start.16 = (bf16[1,3,441]{2,1,0:T(4,128)(2,1)S(1)}, bf16[1,3,441]{2,1,0:T(4,128)(2,1)S(1)}, u32[]{:S(2)}, u32[]{:S(2)}) collective-permute-start(bf16[1,3,441]{2,1,0:T(4,128)(2,1)S(1)} %collective-permute-done.15), channel_id=1, source_target_pairs={{0,16},{16,32},{32,48},{48,64},{64,80},{80,96},{96,112},{112,128},... | collective-permute-start | bytes 7946 | tf_op jit(solution)/shard_map/ppermute | solution.py:161
  121.5 6.9 %collective-permute-start.17 = (bf16[1,3,441]{2,1,0:T(4,128)(2,1)S(1)}, bf16[1,3,441]{2,1,0:T(4,128)(2,1)S(1)}, u32[]{:S(2)}, u32[]{:S(2)}) collective-permute-start(bf16[1,3,441]{2,1,0:T(4,128)(2,1)S(1)} %collective-permute-done.16), channel_id=1, source_target_pairs={{0,16},{16,32},{32,48},{48,64},{64,80},{80,96},{96,112},{112,128},... | collective-permute-start | bytes 7946 | tf_op jit(solution)/shard_map/ppermute | solution.py:161
  128.4 6.9 %collective-permute-start.18 = (bf16[1,3,441]{2,1,0:T(4,128)(2,1)S(1)}, bf16[1,3,441]{2,1,0:T(4,128)(2,1)S(1)}, u32[]{:S(2)}, u32[]{:S(2)}) collective-permute-start(bf16[1,3,441]{2,1,0:T(4,128)(2,1)S(1)} %collective-permute-done.17), channel_id=1, source_target_pairs={{0,16},{16,32},{32,48},{48,64},{64,80},{80,96},{96,112},{112,128},... | collective-permute-start | bytes 7946 | tf_op jit(solution)/shard_map/ppermute | solution.py:161
  135.3 13.0 %collective-permute-start.19 = (bf16[1,3,441]{2,1,0:T(4,128)(2,1)S(1)}, bf16[1,3,441]{2,1,0:T(4,128)(2,1)S(1)}, u32[]{:S(2)}, u32[]{:S(2)}) collective-permute-start(bf16[1,3,441]{2,1,0:T(4,128)(2,1)S(1)} %collective-permute-done.18), channel_id=1, source_target_pairs={{0,16},{16,32},{32,48},{48,64},{64,80},{80,96},{96,112},{112,128},... | collective-permute-start | bytes 7946 | tf_op jit(solution)/shard_map/ppermute | solution.py:161
  148.4 3.9 collective-permute-start.20
  152.2 4.7 collective-permute-start.21
  156.9 33.1 %collective-permute-start.22 = (bf16[1,3,441]{2,1,0:T(4,128)(2,1)}, bf16[1,3,441]{2,1,0:T(4,128)(2,1)}, u32[]{:S(2)}, u32[]{:S(2)}) collective-permute-start(bf16[1,3,441]{2,1,0:T(4,128)(2,1)} %collective-permute-done.21), channel_id=1, source_target_pairs={{0,16},{16,32},{32,48},{48,64},{64,80},{80,96},{96,112},{112,128},... | collective-permute-start | bytes 7946 | tf_op jit(solution)/shard_map/ppermute | solution.py:161
  190.0 7.8 %collective-permute-start.23 = (bf16[1,3,441]{2,1,0:T(4,128)(2,1)}, bf16[1,3,441]{2,1,0:T(4,128)(2,1)}, u32[]{:S(2)}, u32[]{:S(2)}) collective-permute-start(bf16[1,3,441]{2,1,0:T(4,128)(2,1)} %collective-permute-done.22), channel_id=1, source_target_pairs={{0,16},{16,32},{32,48},{48,64},{64,80},{80,96},{96,112},{112,128},... | collective-permute-start | bytes 7946 | tf_op jit(solution)/shard_map/ppermute | solution.py:161
  254.3 31.4 %copy-start.13 = (f32[3,64,128]{2,0,1:T(4,128)}, f32[3,64,128]{2,0,1:T(4,128)S(1)}, u32[]{:S(2)}) copy-start(f32[3,64,128]{2,0,1:T(4,128)S(1)} %fusion.131) | copy-start | bytes 294916
  254.3 30.7 %copy-start.22 = (f32[64,128]{1,0:T(8,128)S(1)}, f32[64,128]{1,0:T(8,128)}, u32[]{:S(2)}) copy-start(f32[64,128]{1,0:T(8,128)} %get-tuple-element.82) | copy-start | bytes 98308
  254.3 30.7 %copy-start.23 = (f32[64,128]{1,0:T(8,128)S(1)}, f32[64,128]{1,0:T(8,128)}, u32[]{:S(2)}) copy-start(f32[64,128]{1,0:T(8,128)} %get-tuple-element.83) | copy-start | bytes 98308
  254.3 30.7 %copy-start.24 = (f32[64,128]{1,0:T(8,128)S(1)}, f32[64,128]{1,0:T(8,128)}, u32[]{:S(2)}) copy-start(f32[64,128]{1,0:T(8,128)} %get-tuple-element.108) | copy-start | bytes 98308
  254.3 30.7 %copy-start.25 = (f32[64,128]{1,0:T(8,128)S(1)}, f32[64,128]{1,0:T(8,128)}, u32[]{:S(2)}) copy-start(f32[64,128]{1,0:T(8,128)} %get-tuple-element.109) | copy-start | bytes 98308
  254.4 30.7 %copy-start.26 = (f32[64,128]{1,0:T(8,128)S(1)}, f32[64,128]{1,0:T(8,128)}, u32[]{:S(2)}) copy-start(f32[64,128]{1,0:T(8,128)} %get-tuple-element.110) | copy-start | bytes 98308
  254.4 31.4 %copy-start.18 = (f32[21,64,128]{2,1,0:T(8,128)S(1)}, f32[21,64,128]{2,1,0:T(8,128)}, u32[]{:S(2)}) copy-start(f32[21,64,128]{2,1,0:T(8,128)} %get-tuple-element.219) | copy-start | bytes 2064388
  255.6 33.4 %copy-start.12 = (f32[3,64,128]{2,0,1:T(4,128)S(1)}, f32[3,64,128]{2,0,1:T(4,128)}, u32[]{:S(2)}) copy-start(f32[3,64,128]{2,0,1:T(4,128)} %copy-done.11) | copy-start | bytes 294916
  309.6 73.8 %copy-start.9 = (bf16[3,1,64,128]{3,2,1,0:T(8,128)(2,1)S(1)}, bf16[3,1,64,128]{3,2,1,0:T(8,128)(2,1)}, u32[]{:S(2)}) copy-start(bf16[3,1,64,128]{3,2,1,0:T(8,128)(2,1)} %copy-done.8) | copy-start | bytes 147460
  309.6 1.2 collective-permute-start.28
  311.1 3.6 collective-permute-start.29
  315.1 4.5 collective-permute-start.30
  320.0 7.7 %collective-permute-start.31 = (bf16[3,441]{1,0:T(4,128)(2,1)S(1)}, bf16[3,441]{1,0:T(4,128)(2,1)S(1)}, u32[]{:S(2)}, u32[]{:S(2)}) collective-permute-start(bf16[3,441]{1,0:T(4,128)(2,1)S(1)} %fusion.249), channel_id=1, source_target_pairs={{0,8},{8,0},{1,9},{9,1},{2,10},{10,2},{3,11},{11,3},{4,12},{12,4},... | collective-permute-start | bytes 7946 | tf_op jit(solution)/shard_map/ppermute | solution.py:37
  327.6 48.9 %copy-start.37 = (bf16[3,441]{1,0:T(4,128)(2,1)}, bf16[3,441]{1,0:T(4,128)(2,1)S(1)}, u32[]{:S(2)}) copy-start(bf16[3,441]{1,0:T(4,128)(2,1)S(1)} %collective-permute-done.31) | copy-start | bytes 7942
  328.0 3.6 collective-permute-start.32
  331.6 4.7 collective-permute-start.33
  336.3 6.9 %collective-permute-start.34 = (bf16[1,3,441]{2,1,0:T(4,128)(2,1)S(1)}, bf16[1,3,441]{2,1,0:T(4,128)(2,1)S(1)}, u32[]{:S(2)}, u32[]{:S(2)}) collective-permute-start(bf16[1,3,441]{2,1,0:T(4,128)(2,1)S(1)} %collective-permute-done.33), channel_id=1, source_target_pairs={{0,16},{16,32},{32,48},{48,64},{64,80},{80,96},{96,112},{112,128},... | collective-permute-start | bytes 7946 | tf_op jit(solution)/shard_map/ppermute | solution.py:161
  343.2 6.9 %collective-permute-start.35 = (bf16[1,3,441]{2,1,0:T(4,128)(2,1)S(1)}, bf16[1,3,441]{2,1,0:T(4,128)(2,1)S(1)}, u32[]{:S(2)}, u32[]{:S(2)}) collective-permute-start(bf16[1,3,441]{2,1,0:T(4,128)(2,1)S(1)} %collective-permute-done.34), channel_id=1, source_target_pairs={{0,16},{16,32},{32,48},{48,64},{64,80},{80,96},{96,112},{112,128},... | collective-permute-start | bytes 7946 | tf_op jit(solution)/shard_map/ppermute | solution.py:161
  350.1 6.9 %collective-permute-start.36 = (bf16[1,3,441]{2,1,0:T(4,128)(2,1)S(1)}, bf16[1,3,441]{2,1,0:T(4,128)(2,1)S(1)}, u32[]{:S(2)}, u32[]{:S(2)}) collective-permute-start(bf16[1,3,441]{2,1,0:T(4,128)(2,1)S(1)} %collective-permute-done.35), channel_id=1, source_target_pairs={{0,16},{16,32},{32,48},{48,64},{64,80},{80,96},{96,112},{112,128},... | collective-permute-start | bytes 7946 | tf_op jit(solution)/shard_map/ppermute | solution.py:161
  357.1 6.9 %collective-permute-start.37 = (bf16[1,3,441]{2,1,0:T(4,128)(2,1)S(1)}, bf16[1,3,441]{2,1,0:T(4,128)(2,1)S(1)}, u32[]{:S(2)}, u32[]{:S(2)}) collective-permute-start(bf16[1,3,441]{2,1,0:T(4,128)(2,1)S(1)} %collective-permute-done.36), channel_id=1, source_target_pairs={{0,16},{16,32},{32,48},{48,64},{64,80},{80,96},{96,112},{112,128},... | collective-permute-start | bytes 7946 | tf_op jit(solution)/shard_map/ppermute | solution.py:161
  364.0 6.9 %collective-permute-start.38 = (bf16[1,3,441]{2,1,0:T(4,128)(2,1)S(1)}, bf16[1,3,441]{2,1,0:T(4,128)(2,1)S(1)}, u32[]{:S(2)}, u32[]{:S(2)}) collective-permute-start(bf16[1,3,441]{2,1,0:T(4,128)(2,1)S(1)} %collective-permute-done.37), channel_id=1, source_target_pairs={{0,16},{16,32},{32,48},{48,64},{64,80},{80,96},{96,112},{112,128},... | collective-permute-start | bytes 7946 | tf_op jit(solution)/shard_map/ppermute | solution.py:161
  370.9 7.4 %collective-permute-start.39 = (bf16[1,3,441]{2,1,0:T(4,128)(2,1)S(1)}, bf16[1,3,441]{2,1,0:T(4,128)(2,1)S(1)}, u32[]{:S(2)}, u32[]{:S(2)}) collective-permute-start(bf16[1,3,441]{2,1,0:T(4,128)(2,1)S(1)} %collective-permute-done.38), channel_id=1, source_target_pairs={{0,16},{16,32},{32,48},{48,64},{64,80},{80,96},{96,112},{112,128},... | collective-permute-start | bytes 7946 | tf_op jit(solution)/shard_map/ppermute | solution.py:161
  378.3 12.4 %collective-permute-start.40 = (bf16[1,3,441]{2,1,0:T(4,128)(2,1)S(1)}, bf16[1,3,441]{2,1,0:T(4,128)(2,1)S(1)}, u32[]{:S(2)}, u32[]{:S(2)}) collective-permute-start(bf16[1,3,441]{2,1,0:T(4,128)(2,1)S(1)} %collective-permute-done.39), channel_id=1, source_target_pairs={{0,16},{16,32},{32,48},{48,64},{64,80},{80,96},{96,112},{112,128},... | collective-permute-start | bytes 7946 | tf_op jit(solution)/shard_map/ppermute | solution.py:161
  385.2 92.4 %collective-permute-start.27 = (bf16[6,1,64,128]{3,2,1,0:T(8,128)(2,1)}, bf16[6,1,64,128]{3,2,1,0:T(8,128)(2,1)}, u32[]{:S(2)}, u32[]{:S(2)}) collective-permute-start(bf16[6,1,64,128]{3,2,1,0:T(8,128)(2,1)} %pad_maximum_fusion.2), channel_id=1, source_target_pairs={{16,0},{32,16},{48,32},{64,48},{80,64},{96,80},{112,96},{128,112},... | collective-permute-start | bytes 294920 | tf_op jit(solution)/shard_map/ppermute | solution.py:25
  385.3 92.3 %collective-permute-start.26 = (bf16[6,1,64,128]{3,2,1,0:T(8,128)(2,1)}, bf16[6,1,64,128]{3,2,1,0:T(8,128)(2,1)}, u32[]{:S(2)}, u32[]{:S(2)}) collective-permute-start(bf16[6,1,64,128]{3,2,1,0:T(8,128)(2,1)} %pad_maximum_fusion.2), channel_id=1, source_target_pairs={{0,16},{16,32},{32,48},{48,64},{64,80},{80,96},{96,112},{112,128},... | collective-permute-start | bytes 294920 | tf_op jit(solution)/shard_map/ppermute | solution.py:24
  390.7 3.6 collective-permute-start.41
  394.3 9.7 %collective-permute-start.42 = (bf16[1,3,441]{2,1,0:T(4,128)(2,1)S(1)}, bf16[1,3,441]{2,1,0:T(4,128)(2,1)S(1)}, u32[]{:S(2)}, u32[]{:S(2)}) collective-permute-start(bf16[1,3,441]{2,1,0:T(4,128)(2,1)S(1)} %collective-permute-done.41), channel_id=1, source_target_pairs={{0,16},{16,32},{32,48},{48,64},{64,80},{80,96},{96,112},{112,128},... | collective-permute-start | bytes 7946 | tf_op jit(solution)/shard_map/ppermute | solution.py:161
  399.6 13.3 %collective-permute-start.25 = (bf16[6,1,1,128]{3,2,1,0:T(2,128)(2,1)S(1)}, bf16[6,1,1,128]{3,2,1,0:T(2,128)(2,1)S(1)}, u32[]{:S(2)}, u32[]{:S(2)}) collective-permute-start(bf16[6,1,1,128]{3,2,1,0:T(2,128)(2,1)S(1)} %get-tuple-element.180), channel_id=1, source_target_pairs={{1,0},{2,1},{3,2},{4,3},{5,4},{6,5},{7,6},{8,7},{9,8},{10,9},{11,1... | collective-permute-start | bytes 4616 | tf_op jit(solution)/shard_map/ppermute | solution.py:25
  400.9 12.0 %collective-permute-start.24 = (bf16[6,1,1,128]{3,2,1,0:T(2,128)(2,1)S(1)}, bf16[6,1,1,128]{3,2,1,0:T(2,128)(2,1)S(1)}, u32[]{:S(2)}, u32[]{:S(2)}) collective-permute-start(bf16[6,1,1,128]{3,2,1,0:T(2,128)(2,1)S(1)} %get-tuple-element.179), channel_id=1, source_target_pairs={{0,1},{1,2},{2,3},{3,4},{4,5},{5,6},{6,7},{7,8},{8,9},{9,10},{10,1... | collective-permute-start | bytes 4616 | tf_op jit(solution)/shard_map/ppermute | solution.py:24
  404.0 6.4 %collective-permute-start.43 = (bf16[1,3,441]{2,1,0:T(4,128)(2,1)S(1)}, bf16[1,3,441]{2,1,0:T(4,128)(2,1)S(1)}, u32[]{:S(2)}, u32[]{:S(2)}) collective-permute-start(bf16[1,3,441]{2,1,0:T(4,128)(2,1)S(1)} %collective-permute-done.42), channel_id=1, source_target_pairs={{0,16},{16,32},{32,48},{48,64},{64,80},{80,96},{96,112},{112,128},... | collective-permute-start | bytes 7946 | tf_op jit(solution)/shard_map/ppermute | solution.py:161
  410.4 3.9 collective-permute-start.44
  414.3 6.9 %collective-permute-start.45 = (bf16[1,3,441]{2,1,0:T(4,128)(2,1)S(1)}, bf16[1,3,441]{2,1,0:T(4,128)(2,1)S(1)}, u32[]{:S(2)}, u32[]{:S(2)}) collective-permute-start(bf16[1,3,441]{2,1,0:T(4,128)(2,1)S(1)} %collective-permute-done.44), channel_id=1, source_target_pairs={{0,16},{16,32},{32,48},{48,64},{64,80},{80,96},{96,112},{112,128},... | collective-permute-start | bytes 7946 | tf_op jit(solution)/shard_map/ppermute | solution.py:161
  421.2 31.2 %collective-permute-start.46 = (bf16[1,3,441]{2,1,0:T(4,128)(2,1)S(1)}, bf16[1,3,441]{2,1,0:T(4,128)(2,1)S(1)}, u32[]{:S(2)}, u32[]{:S(2)}) collective-permute-start(bf16[1,3,441]{2,1,0:T(4,128)(2,1)S(1)} %collective-permute-done.45), channel_id=1, source_target_pairs={{0,16},{16,32},{32,48},{48,64},{64,80},{80,96},{96,112},{112,128},... | collective-permute-start | bytes 7946 | tf_op jit(solution)/shard_map/ppermute | solution.py:161
  477.6 30.1 %copy-start.21 = (f32[3,1,64,128]{3,2,1,0:T(8,128)S(1)}, f32[3,1,64,128]{3,2,1,0:T(8,128)}, u32[]{:S(2)}) copy-start(f32[3,1,64,128]{3,2,1,0:T(8,128)} %get-tuple-element.116) | copy-start | bytes 294916
  477.6 30.1 %copy-start.39 = (f32[64,128]{1,0:T(8,128)S(1)}, f32[64,128]{1,0:T(8,128)}, u32[]{:S(2)}) copy-start(f32[64,128]{1,0:T(8,128)} %get-tuple-element.69) | copy-start | bytes 98308
  477.6 30.1 %copy-start.40 = (f32[64,128]{1,0:T(8,128)S(1)}, f32[64,128]{1,0:T(8,128)}, u32[]{:S(2)}) copy-start(f32[64,128]{1,0:T(8,128)} %get-tuple-element.70) | copy-start | bytes 98308
  477.6 30.1 %copy-start.41 = (f32[64,128]{1,0:T(8,128)S(1)}, f32[64,128]{1,0:T(8,128)}, u32[]{:S(2)}) copy-start(f32[64,128]{1,0:T(8,128)} %get-tuple-element.71) | copy-start | bytes 98308
  (57 other events, 721.6 us)
